TPU v7x, 32 devices: a whole 2x2x4 slice. The times are simulated.
32 devices in a mesh: section: 2 (over x), group: 4 (over y, core), replica: 4 (over z).
Axes of the slice: x: 2, y: 2, z: 4, core: 2. Of those that a mesh axis runs over, the one named last changes fastest.
Arguments:
- chars: bfloat16 [16384, 768], P(('group', 'replica')), may hold values from -6 to 6
- char_codes: int32 [16384], P(('group', 'replica')), may hold values from 0 to 44127, as said below
- mol_cotangent: bfloat16 [4096, 768], P(('group', 'replica')), may hold values from -6 to 6
- attn_norm_gain: bfloat16 [768], P('group'), may hold values from 0.5 to 1.5
- attn_norm_bias: bfloat16 [768], P('group'), may hold values from -1.75 to 1.75
- qkv_weight: bfloat16 [768, 2304], P('group'), may hold values from -0.21875 to 0.21875
- qv_bias: bfloat16 [1536], P('group'), may hold values from -3 to 3
- out_weight: bfloat16 [768, 768], P('group'), may hold values from -0.625 to 0.625
- out_bias: bfloat16 [768], P('group'), may hold values from -1.75 to 1.75
- ffn_norm_gain: bfloat16 [768], P('group'), may hold values from 0.5 to 1.5
- ffn_norm_bias: bfloat16 [768], P('group'), may hold values from -1.75 to 1.75
- ffn_in_weight: bfloat16 [768, 3072], P('group'), may hold values from -0.21875 to 0.21875
- ffn_in_bias: bfloat16 [3072], P('group'), may hold values from -3 to 3
- ffn_out_weight: bfloat16 [3072, 768], P('group'), may hold values from -0.109375 to 0.109375
- ffn_out_bias: bfloat16 [768], P('group'), may hold values from -1.75 to 1.75
- conv_weight: bfloat16 [3072, 768], P('group'), may hold values from -0.109375 to 0.109375
- conv_bias: bfloat16 [768], P('group'), may hold values from -3 to 3
- down_norm_gain: bfloat16 [768], P('group'), may hold values from 0.5 to 1.5
- down_norm_bias: bfloat16 [768], P('group'), may hold values from -1.75 to 1.75
Outputs:
- molecules: bfloat16 [4096, 768], P(('group', 'replica'), 'section')
- chars_grad: bfloat16 [16384, 768], P(('group', 'replica'), 'section')
- grad_attn_norm_gain: float32 [768], P('group')
- grad_attn_norm_bias: float32 [768], P('group')
- grad_qkv_weight: float32 [768, 2304], P('group')
- grad_qv_bias: float32 [1536], P('group')
- grad_out_weight: float32 [768, 768], P('group')
- grad_out_bias: float32 [768], P('group')
- grad_ffn_norm_gain: float32 [768], P('group')
- grad_ffn_norm_bias: float32 [768], P('group')
- grad_ffn_in_weight: float32 [768, 3072], P('group')
- grad_ffn_in_bias: float32 [3072], P('group')
- grad_ffn_out_weight: float32 [3072, 768], P('group')
- grad_ffn_out_bias: float32 [768], P('group')
- grad_conv_weight: float32 [3072, 768], P('group')
- grad_conv_bias: float32 [768], P('group')
- grad_down_norm_gain: float32 [768], P('group')
- grad_down_norm_bias: float32 [768], P('group')
Inputs may be any that keep to these rules, and one draw needn't show every extreme that they name: `char_codes`: each row of 2048 characters holds nonzero codepoints up to its length and 0 after it; every row ends in padding.
All inputs are finite; a program needn't handle non-finite values.
Results may differ from a plain program's by a relative error of at most 0.02.
Values may be sent and summed in bfloat16 or wider, within the bound.
A program may use at most 320 MiB of HBM per device.

v0:
```python
import jax
import jax.numpy as jnp
from jax import lax
from jax.sharding import PartitionSpec as P

D = 768
HEADS = 12
HEAD_DIM = 64
FF = 3072
WIN = 128
KERNEL = 4
MB = 2


norm_eps = 1e-06
mask_value = -10000.0


def from_behind(block, axis, distance):
    devices = range(lax.axis_size(axis))
    route = [(i - distance, i) for i in devices if i - distance in devices]
    return lax.ppermute(block, axis, route)


def swapped(array, axis, distance):
    return lax.ppermute(array, axis, [(i, i ^ 1 << distance) for i in range(lax.axis_size(axis))])


def as_sent(array):

    def short(part):
        return part.astype(jnp.bfloat16) if part.dtype == jnp.float32 else part

    return jax.tree.map(short, array)


def layer_norm(values, norm_gain, norm_shift):
    center = values - jnp.mean(values, axis=-1, keepdims=True)
    spread = jnp.mean(center * center, axis=-1, keepdims=True)
    return center * lax.rsqrt(spread + norm_eps) * norm_gain + norm_shift


def gelu_exact(values):
    return jax.nn.gelu(values, approximate=False)


def project(left_side, right_side):
    return jnp.dot(left_side, right_side, preferred_element_type=jnp.float32)


def contract_rows(left_side, right_side):
    return lax.dot_general(
        left_side, right_side, (((0,), (0,)), ((), ())), preferred_element_type=jnp.float32
    )


def times_transpose(left_side, right_side):
    return lax.dot_general(
        left_side, right_side, (((1,), (1,)), ((), ())), preferred_element_type=jnp.float32
    )


def norm_back(values, norm_gain, norm_shift, grad_out):
    outputs, pullback = jax.vjp(layer_norm, values, norm_gain, norm_shift)
    return pullback(grad_out)


def window_bias(row_codes):
    windows = row_codes.shape[0] // WIN
    return (
        jnp.where(row_codes != 0, 0.0, mask_value).astype(jnp.float32).reshape(windows, 1, 1, WIN)
    )


def attention_scores(queries, keys_all, key_bias):
    raw_scores = jnp.einsum(
        "wqhd,wkhd->whqk", queries, keys_all, preferred_element_type=jnp.float32
    )
    return raw_scores * HEAD_DIM ** (-0.5) + key_bias


def rows_of(array, index, count):
    return array[index * count : (index + 1) * count]


def kept_zeros(row_count):
    windows = row_count // WIN
    return (
        jnp.zeros((row_count, D), jnp.bfloat16),
        jnp.zeros((row_count, 3 * D), jnp.bfloat16),
        jnp.zeros((windows, HEADS, WIN, 1), jnp.float32),
        jnp.zeros((row_count, D), jnp.bfloat16),
        jnp.zeros((row_count, D), jnp.float32),
        jnp.zeros((row_count, D), jnp.bfloat16),
        jnp.zeros((row_count, FF), jnp.float32),
        jnp.zeros((row_count, FF), jnp.bfloat16),
    )


def first_forward(weights, row_chars, row_codes):
    (
        attn_norm_gain,
        attn_norm_bias,
        qkv_weight,
        qv_bias,
        out_weight,
        out_bias,
        ffn_norm_gain,
        ffn_norm_bias,
        ffn_in_weight,
        ffn_in_bias,
        ffn_out_weight,
        ffn_out_bias,
    ) = weights[:12]
    row_count = row_chars.shape[0]
    windows = row_count // WIN
    chars_wide = row_chars.astype(jnp.float32)
    normed = layer_norm(
        chars_wide, attn_norm_gain.astype(jnp.float32), attn_norm_bias.astype(jnp.float32)
    ).astype(jnp.bfloat16)
    bias_row = jnp.concatenate([qv_bias[:D], jnp.zeros((D,), jnp.bfloat16), qv_bias[D:]]).astype(
        jnp.float32
    )
    projected = (project(normed, qkv_weight) + bias_row).astype(jnp.bfloat16)
    heads_split = projected.reshape(windows, WIN, 3, HEADS, HEAD_DIM)
    scores = attention_scores(heads_split[:, :, 0], heads_split[:, :, 1], window_bias(row_codes))
    top_score = jnp.max(scores, axis=-1, keepdims=True)
    log_total = top_score + jnp.log(jnp.sum(jnp.exp(scores - top_score), axis=-1, keepdims=True))
    prob_weights = jnp.exp(scores - log_total).astype(jnp.bfloat16)
    context = jnp.einsum(
        "whqk,wkhd->wqhd", prob_weights, heads_split[:, :, 2], preferred_element_type=jnp.float32
    )
    context = context.reshape(row_count, D).astype(jnp.bfloat16)
    hidden = chars_wide + project(context, out_weight) + out_bias.astype(jnp.float32)
    normed_ffn = layer_norm(
        hidden, ffn_norm_gain.astype(jnp.float32), ffn_norm_bias.astype(jnp.float32)
    ).astype(jnp.bfloat16)
    inner_act = project(normed_ffn, ffn_in_weight) + ffn_in_bias.astype(jnp.float32)
    active = gelu_exact(inner_act).astype(jnp.bfloat16)
    layer_out = hidden + project(active, ffn_out_weight) + ffn_out_bias.astype(jnp.float32)
    kept = (normed, projected, log_total, context, hidden, normed_ffn, inner_act, active)
    return (layer_out.astype(jnp.bfloat16), kept)


def first_backward(weights, row_chars, row_codes, kept, grad_out):
    (
        attn_norm_gain,
        attn_norm_bias,
        qkv_weight,
        qv_bias,
        out_weight,
        out_bias,
        ffn_norm_gain,
        ffn_norm_bias,
        ffn_in_weight,
        ffn_in_bias,
        ffn_out_weight,
        ffn_out_bias,
    ) = weights[:12]
    normed, projected, log_total, context, hidden, normed_ffn, inner_act, active = kept
    row_count = row_chars.shape[0]
    windows = row_count // WIN
    grad_layer = grad_out.astype(jnp.float32)
    grad_ffn_out_weight = contract_rows(active, grad_out)
    grad_ffn_out_bias = jnp.sum(grad_layer, axis=0)
    grad_active = times_transpose(grad_out, ffn_out_weight)
    gelu_value, gelu_pull = jax.vjp(gelu_exact, inner_act)
    grad_inner = gelu_pull(grad_active)[0].astype(jnp.bfloat16)
    grad_ffn_in_weight = contract_rows(normed_ffn, grad_inner)
    grad_ffn_in_bias = jnp.sum(grad_inner.astype(jnp.float32), axis=0)
    grad_hidden_norm, grad_ffn_norm_gain, grad_ffn_norm_bias = norm_back(
        hidden,
        ffn_norm_gain.astype(jnp.float32),
        ffn_norm_bias.astype(jnp.float32),
        times_transpose(grad_inner, ffn_in_weight),
    )
    grad_hidden = grad_layer + grad_hidden_norm
    grad_attended = grad_hidden.astype(jnp.bfloat16)
    grad_out_weight = contract_rows(context, grad_attended)
    grad_out_bias = jnp.sum(grad_attended.astype(jnp.float32), axis=0)
    grad_context = times_transpose(grad_attended, out_weight).astype(jnp.bfloat16)
    grad_context = grad_context.reshape(windows, WIN, HEADS, HEAD_DIM)
    heads_split = projected.reshape(windows, WIN, 3, HEADS, HEAD_DIM)
    queries = heads_split[:, :, 0]
    keys_all = heads_split[:, :, 1]
    values_all = heads_split[:, :, 2]
    scores = attention_scores(queries, keys_all, window_bias(row_codes))
    prob_exact = jnp.exp(scores - log_total)
    prob_weights = prob_exact.astype(jnp.bfloat16)
    grad_probs = jnp.einsum(
        "wqhd,wkhd->whqk", grad_context, values_all, preferred_element_type=jnp.float32
    )
    grad_values = jnp.einsum(
        "whqk,wqhd->wkhd", prob_weights, grad_context, preferred_element_type=jnp.float32
    )
    row_inner = jnp.sum(prob_exact * grad_probs, axis=-1, keepdims=True)
    grad_scores = (prob_exact * (grad_probs - row_inner)).astype(jnp.bfloat16)
    scale_factor = HEAD_DIM ** (-0.5)
    grad_queries = (
        jnp.einsum("whqk,wkhd->wqhd", grad_scores, keys_all, preferred_element_type=jnp.float32)
        * scale_factor
    )
    grad_keys = (
        jnp.einsum("whqk,wqhd->wkhd", grad_scores, queries, preferred_element_type=jnp.float32)
        * scale_factor
    )
    grad_projected = jnp.stack([grad_queries, grad_keys, grad_values], axis=2).astype(jnp.bfloat16)
    grad_projected = grad_projected.reshape(row_count, 3 * D)
    grad_qkv_weight = contract_rows(normed, grad_projected)
    column_sums = jnp.sum(grad_projected.astype(jnp.float32), axis=0)
    grad_qv_bias = jnp.concatenate([column_sums[:D], column_sums[2 * D :]])
    grad_chars_norm, grad_attn_norm_gain, grad_attn_norm_bias = norm_back(
        row_chars.astype(jnp.float32),
        attn_norm_gain.astype(jnp.float32),
        attn_norm_bias.astype(jnp.float32),
        times_transpose(grad_projected, qkv_weight),
    )
    grad_chars = grad_hidden + grad_chars_norm
    return (
        grad_chars,
        (
            grad_attn_norm_gain,
            grad_attn_norm_bias,
            grad_qkv_weight,
            grad_qv_bias,
            grad_out_weight,
            grad_out_bias,
            grad_ffn_norm_gain,
            grad_ffn_norm_bias,
            grad_ffn_in_weight,
            grad_ffn_in_bias,
            grad_ffn_out_weight,
            grad_ffn_out_bias,
        ),
    )


def second_layer(weights, handed, cotangent):
    conv_weight, conv_bias, down_norm_gain, down_norm_bias = weights[12:]
    row_count = handed.shape[0]
    stacked = handed.reshape(row_count // KERNEL, KERNEL * D)
    conv_out = project(stacked, conv_weight) + conv_bias.astype(jnp.float32)

    def tail_part(values, norm_gain, norm_shift):
        return layer_norm(gelu_exact(values), norm_gain, norm_shift)

    mol_values, pullback = jax.vjp(
        tail_part, conv_out, down_norm_gain.astype(jnp.float32), down_norm_bias.astype(jnp.float32)
    )
    grad_conv, grad_down_norm_gain, grad_down_norm_bias = pullback(cotangent.astype(jnp.float32))
    grad_conv = grad_conv.astype(jnp.bfloat16)
    grad_conv_weight = contract_rows(stacked, grad_conv)
    grad_conv_bias = jnp.sum(grad_conv.astype(jnp.float32), axis=0)
    grad_handed = times_transpose(grad_conv, conv_weight).astype(jnp.bfloat16).reshape(row_count, D)
    return (
        mol_values.astype(jnp.bfloat16),
        grad_handed,
        (grad_conv_weight, grad_conv_bias, grad_down_norm_gain, grad_down_norm_bias),
    )


def body(
    chars,
    char_codes,
    mol_cotangent,
    attn_norm_gain,
    attn_norm_bias,
    qkv_weight,
    qv_bias,
    out_weight,
    out_bias,
    ffn_norm_gain,
    ffn_norm_bias,
    ffn_in_weight,
    ffn_in_bias,
    ffn_out_weight,
    ffn_out_bias,
    conv_weight,
    conv_bias,
    down_norm_gain,
    down_norm_bias,
):
    weights = (
        lax.all_gather(attn_norm_gain, "group", axis=0, tiled=True),
        lax.all_gather(attn_norm_bias, "group", axis=0, tiled=True),
        lax.all_gather(qkv_weight, "group", axis=0, tiled=True),
        lax.all_gather(qv_bias, "group", axis=0, tiled=True),
        lax.all_gather(out_weight, "group", axis=0, tiled=True),
        lax.all_gather(out_bias, "group", axis=0, tiled=True),
        lax.all_gather(ffn_norm_gain, "group", axis=0, tiled=True),
        lax.all_gather(ffn_norm_bias, "group", axis=0, tiled=True),
        lax.all_gather(ffn_in_weight, "group", axis=0, tiled=True),
        lax.all_gather(ffn_in_bias, "group", axis=0, tiled=True),
        lax.all_gather(ffn_out_weight, "group", axis=0, tiled=True),
        lax.all_gather(ffn_out_bias, "group", axis=0, tiled=True),
        lax.all_gather(conv_weight, "group", axis=0, tiled=True),
        lax.all_gather(conv_bias, "group", axis=0, tiled=True),
        lax.all_gather(down_norm_gain, "group", axis=0, tiled=True),
        lax.all_gather(down_norm_bias, "group", axis=0, tiled=True),
    )
    first_sums = tuple((jnp.zeros(weight.shape, jnp.float32) for weight in weights[:12]))
    last_sums = tuple((jnp.zeros(weight.shape, jnp.float32) for weight in weights[12:]))
    is_first = lax.axis_index("section") == 0
    half_width = D // 2
    mb_rows = chars.shape[0] // MB
    mol_rows = mb_rows // KERNEL
    inbound = jnp.zeros((mb_rows, D), jnp.bfloat16)
    kept_store = []
    grad_pieces = []
    mol_pieces = []
    for tick_index in range(MB + 2):
        forward_index = tick_index if tick_index < MB else -1
        back_index = tick_index - 2
        down_index = tick_index - 1 if tick_index <= MB else -1

        def first_section():
            outbound = jnp.zeros((mb_rows, D), jnp.bfloat16)
            kept_new = None
            grad_rows = None
            updated = first_sums
            if forward_index >= 0:
                outbound, kept_new = first_forward(
                    weights,
                    rows_of(chars, forward_index, mb_rows),
                    rows_of(char_codes, forward_index, mb_rows),
                )
            if back_index >= 0:
                grad_rows, increments = first_backward(
                    weights,
                    rows_of(chars, back_index, mb_rows),
                    rows_of(char_codes, back_index, mb_rows),
                    kept_store[back_index],
                    inbound,
                )
                updated = jax.tree.map(jnp.add, updated, increments)
            mol_new = jnp.zeros((mol_rows, D), jnp.bfloat16) if down_index >= 0 else None
            return (outbound, updated, last_sums, kept_new, grad_rows, mol_new)

        def last_section():
            outbound = jnp.zeros((mb_rows, D), jnp.bfloat16)
            updated = last_sums
            mol_new = None
            if down_index >= 0:
                mol_new, outbound, increments = second_layer(
                    weights, inbound, rows_of(mol_cotangent, down_index, mol_rows)
                )
                updated = jax.tree.map(jnp.add, updated, increments)
            kept_new = kept_zeros(mb_rows) if forward_index >= 0 else None
            grad_rows = jnp.zeros((mb_rows, D), jnp.float32) if back_index >= 0 else None
            return (outbound, first_sums, updated, kept_new, grad_rows, mol_new)

        outbound, first_sums, last_sums, kept_new, grad_rows, mol_new = lax.cond(
            is_first, first_section, last_section
        )
        if forward_index >= 0:
            kept_store.append(kept_new)
        if back_index >= 0:
            grad_pieces.append(grad_rows)
        if down_index >= 0:
            mol_pieces.append(mol_new)
        if tick_index <= MB:
            empty_rows = jnp.zeros((mb_rows, D), jnp.bfloat16)
            from_below = from_behind(outbound, "section", 1) if tick_index < MB else empty_rows
            from_above = from_behind(outbound, "section", -1) if tick_index >= 1 else empty_rows
            inbound = jnp.where(is_first, from_above, from_below)
    grad_whole = jnp.concatenate(grad_pieces, axis=0).astype(jnp.bfloat16)
    mol_whole = jnp.concatenate(mol_pieces, axis=0)
    other_grad, other_mol = swapped(
        (grad_whole[:, half_width:], mol_whole[:, :half_width]), "section", 0
    )
    chars_grad = jnp.where(is_first, grad_whole[:, :half_width], other_grad)
    molecules = jnp.where(is_first, other_mol, mol_whole[:, half_width:])
    all_sums = first_sums + last_sums
    shard_sums = jax.tree.map(
        lambda part: part.astype(jnp.float32),
        lax.psum_scatter(as_sent(all_sums), "group", scatter_dimension=0, tiled=True),
    )
    totals = lax.psum(shard_sums, ("section", "replica"))
    return (molecules, chars_grad) + tuple(totals)


def solution(mesh):
    return jax.shard_map(
        body,
        mesh=mesh,
        in_specs=(
            P(("group", "replica"), None),
            P(("group", "replica")),
            P(("group", "replica"), None),
            P("group"),
            P("group"),
            P("group", None),
            P("group"),
            P("group", None),
            P("group"),
            P("group"),
            P("group"),
            P("group", None),
            P("group"),
            P("group", None),
            P("group"),
            P("group", None),
            P("group"),
            P("group"),
            P("group"),
        ),
        out_specs=(
            P(("group", "replica"), "section"),
            P(("group", "replica"), "section"),
            P("group"),
            P("group"),
            P("group", None),
            P("group"),
            P("group", None),
            P("group"),
            P("group"),
            P("group"),
            P("group", None),
            P("group"),
            P("group", None),
            P("group"),
            P("group", None),
            P("group"),
            P("group"),
            P("group"),
        ),
        check_vma=False,
    )
```

profile of v0, /device:TPU:0, one launch (start us, length us, event | category | flops | bytes accessed | tf_op | source)
XLA Modules:
  0.0 1119.2 jit_solution(13957427149708810296)
XLA Ops:
  25.9 12.3 %all-reduce.22 = (bf16[768]{0:T(1024)(128)(2,1)}, bf16[768]{0:T(1024)(128)(2,1)}, bf16[768]{0:T(1024)(128)(2,1)}, bf16[768]{0:T(1024)(128)(2,1)S(1)}, bf16[768]{...) all-reduce(bf16[768]{0:T(1024)(128)(2,1)S(1)} %dynamic-update-slice, ...), channel_id=1, replica_groups=mesh['section'=2,'group'=4,'replica'=4] {'group'}, use_global_device_ids=true, to_apply=%add | all-reduce | flops 6912 | bytes 27648
  38.2 24.1 %all-gather.8.cloned.1.call-done = bf16[768,2304]{1,0:T(8,128)(2,1)} async-done(((bf16[192,2304]{1,0:T(8,128)(2,1)}), bf16[768,2304]{1,0:T(8,128)(2,1)}) %all-gather.8.cloned.1.call-update) | async-done | bytes 3538960 | tf_op jit(solution)/shard_map/all_gather | solution.py:286
  62.3 39.1 %all-gather.12.cloned.1.call-done = bf16[768,3072]{1,0:T(8,128)(2,1)} async-done(((bf16[192,3072]{1,0:T(8,128)(2,1)}), bf16[768,3072]{1,0:T(8,128)(2,1)}) %all-gather.12.cloned.1.call-update) | async-done | bytes 4718608 | tf_op jit(solution)/shard_map/all_gather | solution.py:292
  101.4 38.9 %all-gather.14.cloned.1.call-done = bf16[3072,768]{1,0:T(8,128)(2,1)} async-done(((bf16[768,768]{1,0:T(8,128)(2,1)}), bf16[3072,768]{1,0:T(8,128)(2,1)}) %all-gather.14.cloned.1.call-update) | async-done | bytes 4718608 | tf_op jit(solution)/shard_map/all_gather | solution.py:294
  140.3 56.7 %conditional.4 = (bf16[512,768]{1,0:T(8,128)(2,1)S(1)}, bf16[512,768]{1,0:T(8,128)(2,1)S(1)}, bf16[512,2304]{1,0:T(8,128)(2,1)}, f32[4,12,128,1]{2,1,0,3:T(8,128...) conditional(s32[]{:T(128)} %convert_element_type.357, () %tuple.40, ...), branch_computations={%region_0.0_spmd, %region_1.8_spmd} | conditional | flops 7574930432 | bytes 115973552 | solution.py:352
  172.1 19.5 %fusion.2 = (bf16[512,3072]{1,0:T(8,128)(2,1)}, f32[512,3072]{1,0:T(8,128)}) fusion(f32[3072]{0:T(1024)S(1)} %convert_element_type.258, bf16[512,768]{1,0:T(8,128)(2,1)} %add_convert_fusion.1, bf16[768,3072]{1,0:T(8,128)(2,1)S(1)} %bitcast.235), kind=kOutput, calls=%fused_computation.3 | convolution fusion | flops 2519728128 | bytes 14954496 | tf_op jit(solution)/shard_map/cond/branch_1_fun/dot_general | solution.py:48
  199.3 17.4 %collective-permute-done = bf16[512,768]{1,0:T(8,128)(2,1)S(1)} collective-permute-done((bf16[512,768]{1,0:T(8,128)(2,1)S(1)}, bf16[512,768]{1,0:T(8,128)(2,1)S(1)}, u32[]{:S(2)}, u32[]{:S(2)}) %collective-permute-start) | collective-permute-done | bytes 786464 | tf_op jit(solution)/shard_map/ppermute | solution.py:22
  217.6 56.1 %conditional.5 = (bf16[512,768]{1,0:T(8,128)(2,1)S(1)}, f32[3072,768]{1,0:T(8,128)}, f32[768]{0:T(1024)S(1)}, f32[768]{0:T(1024)S(1)}, f32[768]{0:T(1024)S(1)}, ...) conditional(s32[]{:T(128)} %convert_element_type.357, ...), branch_computations={%region_8.16_spmd, %region_16.23_spmd} | conditional | flops 7574930432 | bytes 131908088 | solution.py:352
  245.6 18.3 %fusion.41 = (bf16[512,3072]{1,0:T(8,128)(2,1)}, f32[512,3072]{1,0:T(8,128)}) fusion(f32[3072]{0:T(1024)S(1)} %convert_element_type.284, bf16[512,768]{1,0:T(8,128)(2,1)S(1)} %add_convert_fusion.5, bf16[768,3072]{1,0:T(8,128)(2,1)S(1)} %bitcast.237), kind=kOutput, calls=%fused_computation.99 | convolution fusion | flops 2519728128 | bytes 14954496 | tf_op jit(solution)/shard_map/cond/branch_1_fun/dot_general | solution.py:48
  279.6 15.1 %collective-permute-done.1 = bf16[512,768]{1,0:T(8,128)(2,1)S(1)} collective-permute-done((bf16[512,768]{1,0:T(8,128)(2,1)S(1)}, bf16[512,768]{1,0:T(8,128)(2,1)S(1)}, u32[]{:S(2)}, u32[]{:S(2)}) %collective-permute-start.1) | collective-permute-done | bytes 786464 | tf_op jit(solution)/shard_map/ppermute | solution.py:22
  297.0 92.5 %conditional.6 = (bf16[512,768]{1,0:T(8,128)(2,1)}, f32[768]{0:T(1024)S(1)}, f32[768]{0:T(1024)S(1)}, f32[768,2304]{0,1:T(8,128)}, f32[1536]{0:T(1024)S(1)}, /*i...) conditional(s32[]{:T(128)} %convert_element_type.357, ...), branch_computations={%region_23.31_spmd, %region_31.49_spmd} | conditional | flops 15152572416 | bytes 263945920 | solution.py:352
  300.5 18.6 %convert_reduce_fusion.6 = (f32[3072]{0:T(1024)S(1)}, bf16[512,3072]{1,0:T(8,128)(2,1)S(1)}) fusion(f32[512,3072]{1,0:T(8,128)} %get-tuple-element.261, bf16[512,768]{1,0:T(8,128)(2,1)} %get-tuple-element.260, bf16[3072,768]{1,0:T(8,128)(2,1)} %get-tuple-element.262), kind=kOutput, calls=%fused_computation.198 | convolution fusion | flops 2532307968 | bytes 14954496 | tf_op jit(solution)/shard_map/cond/branch_1_fun/dot_general | solution.py:58
  390.9 18.8 %collective-permute-done.4 = bf16[512,768]{1,0:T(8,128)(2,1)S(1)} collective-permute-done((bf16[512,768]{1,0:T(8,128)(2,1)}, bf16[512,768]{1,0:T(8,128)(2,1)S(1)}, u32[]{:S(2)}, u32[]{:S(2)}) %collective-permute-start.4) | collective-permute-done | bytes 786464 | tf_op jit(solution)/shard_map/ppermute | solution.py:22
  409.7 108.5 %conditional.7 = (f32[768]{0:T(1024)S(1)}, f32[768]{0:T(1024)S(1)}, f32[768,2304]{0,1:T(8,128)}, f32[1536]{0:T(1024)S(1)}, f32[768,768]{0,1:T(8,128)}, /*index=5...) conditional(s32[]{:T(128)} %convert_element_type.357, ...), branch_computations={%region_49.50_spmd, %region_50.68_spmd} | conditional | flops 15160448000 | bytes 303206112 | solution.py:352
  410.7 19.4 %convert_reduce_fusion.11 = (f32[3072]{0:T(1024)S(1)}, bf16[512,3072]{1,0:T(8,128)(2,1)}) fusion(f32[512,3072]{1,0:T(8,128)} %get-tuple-element.295, bf16[512,768]{1,0:T(8,128)(2,1)S(1)} %get-tuple-element.842, bf16[3072,768]{1,0:T(8,128)(2,1)} %get-tuple-element.296), kind=kOutput, calls=%fused_computation.282 | convolution fusion | flops 2532307968 | bytes 14954496 | tf_op jit(solution)/shard_map/cond/branch_1_fun/dot_general | solution.py:58
  469.3 8.7 bitcast_add_fusion.3
  489.6 9.6 copy.150
  507.7 9.6 copy.166
  556.2 10.9 all-reduce.21
  573.2 15.9 %reduce-scatter.6.cloned.1.call-done = bf16[192,2304]{1,0:T(8,128)(2,1)} async-done(((bf16[768,2304]{1,0:T(8,128)(2,1)}), bf16[192,2304]{1,0:T(8,128)(2,1)}) %reduce-scatter.6.cloned.1.call-update) | async-done | bytes 884752 | tf_op jit(solution)/shard_map/reduce_scatter | solution.py:376
  589.2 50.4 %reduce-scatter.14.cloned.1.call-done = bf16[768,768]{1,0:T(8,128)(2,1)} async-done(((bf16[3072,768]{1,0:T(8,128)(2,1)}), bf16[768,768]{1,0:T(8,128)(2,1)}) %reduce-scatter.14.cloned.1.call-update) | async-done | bytes 1179664 | tf_op jit(solution)/shard_map/reduce_scatter | solution.py:376
  639.6 50.6 %reduce-scatter.10.cloned.1.call-done = bf16[192,3072]{1,0:T(8,128)(2,1)} async-done(((bf16[768,3072]{1,0:T(8,128)(2,1)}), bf16[192,3072]{1,0:T(8,128)(2,1)}) %reduce-scatter.10.cloned.1.call-update) | async-done | bytes 1179664 | tf_op jit(solution)/shard_map/reduce_scatter | solution.py:376
  690.1 50.3 %reduce-scatter.12.cloned.1.call-done = bf16[768,768]{1,0:T(8,128)(2,1)} async-done(((bf16[3072,768]{1,0:T(8,128)(2,1)}), bf16[768,768]{1,0:T(8,128)(2,1)}) %reduce-scatter.12.cloned.1.call-update) | async-done | bytes 1179664 | tf_op jit(solution)/shard_map/reduce_scatter | solution.py:376
  740.4 371.5 %all-reduce.24 = (f32[192]{0:T(256)}, f32[192]{0:T(256)}, f32[192,2304]{1,0:T(8,128)}, f32[384]{0:T(512)}, f32[192,768]{1,0:T(8,128)}, /*index=5*/f32[192]{0:T(2...) all-reduce(f32[192]{0:T(256)S(1)} %dynamic-slice_convert_fusion.10,, ...), channel_id=1, replica_groups=mesh['section'=2,'group'=4,'replica'=4] {'section','replica'}, use_global_device_ids=true, to_apply=%region_69.70 | all-reduce | flops 2362176 | bytes 14178816 | tf_op jit(solution)/shard_map/psum | solution.py:378
  (440 shorter events, 280.0 us)
Async XLA Ops:
  7.3 133.0 %copy-start = (bf16[1024,768]{1,0:T(8,128)(2,1)S(1)}, bf16[1024,768]{1,0:T(8,128)(2,1)}, u32[]{:S(2)}) copy-start(bf16[1024,768]{1,0:T(8,128)(2,1)} %param.27) | copy-start | bytes 4718596
  7.3 30.9 %all-gather.10.cloned.1.call-start = ((), (), s32[]{:S(2)}) async-start(), calls=%async_computation.6 | async-start | bytes 1474560 | tf_op jit(solution)/shard_map/all_gather | solution.py:288
  8.1 54.2 %all-gather.8.cloned.1.call-start = ((), (), s32[]{:S(2)}) async-start(), calls=%async_computation.5 | async-start | bytes 4423680 | tf_op jit(solution)/shard_map/all_gather | solution.py:286
  8.8 92.5 %all-gather.12.cloned.1.call-start = ((), (), s32[]{:S(2)}) async-start(), calls=%async_computation.7 | async-start | bytes 5898240 | tf_op jit(solution)/shard_map/all_gather | solution.py:292
  9.5 130.7 %all-gather.14.cloned.1.call-start = ((), (), s32[]{:S(2)}) async-start(), calls=%async_computation.8 | async-start | bytes 5898240 | tf_op jit(solution)/shard_map/all_gather | solution.py:294
  10.1 189.2 %all-gather.16.cloned.1.call-start = ((), (), s32[]{:S(2)}) async-start(), calls=%async_computation.9 | async-start | bytes 5898240 | tf_op jit(solution)/shard_map/all_gather | solution.py:296
  10.7 562.5 %reduce-scatter.8.cloned.1.call-start = ((), (), s32[]{:S(2)}) async-start(), calls=%async_computation.11 | async-start | bytes 1474560 | tf_op jit(solution)/shard_map/reduce_scatter | solution.py:376
  38.2 179.4 %copy-start.47 = (bf16[768]{0:T(1024)(128)(2,1)}, bf16[768]{0:T(1024)(128)(2,1)S(1)}, u32[]{:S(2)}) copy-start(bf16[768]{0:T(1024)(128)(2,1)S(1)} %get-tuple-element.817) | copy-start | bytes 4612
  140.3 77.4 %copy-start.16 = (bf16[256,768]{1,0:T(8,128)(2,1)S(1)}, bf16[256,768]{1,0:T(8,128)(2,1)}, u32[]{:S(2)}) copy-start(bf16[256,768]{1,0:T(8,128)(2,1)} %param.29) | copy-start | bytes 1179652
  169.3 22.3 %slice-start.6 = ((s8[4718592]{0:T(1024)(128)(4,1)}), s8[4194304]{0:T(1024)(128)(4,1)S(1)}, s32[]{:S(2)}) async-start(s8[4718592]{0:T(1024)(128)(4,1)} %bitcast.238), calls=%async_computation.21 | async-start | bytes 8388608 | tf_op jit(solution)/shard_map/cond
  197.9 18.8 %collective-permute-start = (bf16[512,768]{1,0:T(8,128)(2,1)S(1)}, bf16[512,768]{1,0:T(8,128)(2,1)S(1)}, u32[]{:S(2)}, u32[]{:S(2)}) collective-permute-start(bf16[512,768]{1,0:T(8,128)(2,1)S(1)} %get-tuple-element.391), channel_id=1, source_target_pairs={{0,16},{1,17},{2,18},{3,19},{4,20},{5,21},{6,22},{7,23},{8,24},{9,... | collective-permute-start | bytes 2359304 | tf_op jit(solution)/shard_map/ppermute | solution.py:22
  243.3 20.6 %copy-start.1 = (f32[512,768]{1,0:T(8,128)}, f32[512,768]{1,0:T(8,128)S(1)}, u32[]{:S(2)}) copy-start(f32[512,768]{1,0:T(8,128)S(1)} %get-tuple-element.958) | copy-start | bytes 4718596 | tf_op jit(solution)/shard_map/cond
  243.7 20.2 %slice-start.8 = ((s8[4718592]{0:T(1024)(128)(4,1)}), s8[4194304]{0:T(1024)(128)(4,1)S(1)}, s32[]{:S(2)}) async-start(s8[4718592]{0:T(1024)(128)(4,1)} %bitcast.240), calls=%async_computation.23 | async-start | bytes 8388608 | tf_op jit(solution)/shard_map/cond
  273.7 21.1 %collective-permute-start.1 = (bf16[512,768]{1,0:T(8,128)(2,1)S(1)}, bf16[512,768]{1,0:T(8,128)(2,1)S(1)}, u32[]{:S(2)}, u32[]{:S(2)}) collective-permute-start(bf16[512,768]{1,0:T(8,128)(2,1)S(1)} %get-tuple-element.393), channel_id=1, source_target_pairs={{16,0},{17,1},{18,2},{19,3},{20,4},{21,5},{22,6},{23,7},{24,8},{25... | collective-permute-start | bytes 2359304 | tf_op jit(solution)/shard_map/ppermute | solution.py:22
  275.0 21.0 %collective-permute-start.2 = (bf16[512,768]{1,0:T(8,128)(2,1)S(1)}, bf16[512,768]{1,0:T(8,128)(2,1)S(1)}, u32[]{:S(2)}, u32[]{:S(2)}) collective-permute-start(bf16[512,768]{1,0:T(8,128)(2,1)S(1)} %get-tuple-element.393), channel_id=1, source_target_pairs={{0,16},{1,17},{2,18},{3,19},{4,20},{5,21},{6,22},{7,23},{8,24},{9,... | collective-permute-start | bytes 2359304 | tf_op jit(solution)/shard_map/ppermute | solution.py:22
  297.0 112.7 %copy-start.2 = (f32[512,768]{1,0:T(8,128)S(1)}, f32[512,768]{1,0:T(8,128)}, u32[]{:S(2)}) copy-start(f32[512,768]{1,0:T(8,128)} %get-tuple-element.424) | copy-start | bytes 4718596
  389.5 20.1 %copy-start.43 = (f32[768]{0:T(1024)}, f32[768]{0:T(1024)S(1)}, u32[]{:S(2)}) copy-start(f32[768]{0:T(1024)S(1)} %get-tuple-element.419) | copy-start | bytes 9220
  389.6 20.1 %collective-permute-start.4 = (bf16[512,768]{1,0:T(8,128)(2,1)}, bf16[512,768]{1,0:T(8,128)(2,1)S(1)}, u32[]{:S(2)}, u32[]{:S(2)}) collective-permute-start(bf16[512,768]{1,0:T(8,128)(2,1)} %get-tuple-element.422), channel_id=1, source_target_pairs={{16,0},{17,1},{18,2},{19,3},{20,4},{21,5},{22,6},{23,7},{24,8},{25... | collective-permute-start | bytes 2359304 | tf_op jit(solution)/shard_map/ppermute | solution.py:22
  520.9 68.3 %reduce-scatter.6.cloned.1.call-start = ((), (), s32[]{:S(2)}) async-start(), calls=%async_computation.10 | async-start | bytes 4423680 | tf_op jit(solution)/shard_map/reduce_scatter | solution.py:376
  527.6 111.9 %reduce-scatter.14.cloned.1.call-start = ((), (), s32[]{:S(2)}) async-start(), calls=%async_computation.14 | async-start | bytes 5898240 | tf_op jit(solution)/shard_map/reduce_scatter | solution.py:376
  534.1 156.0 %reduce-scatter.10.cloned.1.call-start = ((), (), s32[]{:S(2)}) async-start(), calls=%async_computation.12 | async-start | bytes 5898240 | tf_op jit(solution)/shard_map/reduce_scatter | solution.py:376
  542.0 198.5 %reduce-scatter.12.cloned.1.call-start = ((), (), s32[]{:S(2)}) async-start(), calls=%async_computation.13 | async-start | bytes 5898240 | tf_op jit(solution)/shard_map/reduce_scatter | solution.py:376
  549.4 5.7 collective-permute-start.3
  556.1 16.2 %collective-permute-start.5 = (bf16[1024,384]{1,0:T(8,128)(2,1)S(1)}, bf16[1024,384]{1,0:T(8,128)(2,1)S(1)}, u32[]{:S(2)}, u32[]{:S(2)}) collective-permute-start(bf16[1024,384]{1,0:T(8,128)(2,1)S(1)} %slice.169), channel_id=1, source_target_pairs={{0,16},{16,0},{1,17},{17,1},{2,18},{18,2},{3,19},{19,3},{4,20},{20... | collective-permute-start | bytes 2359304 | tf_op jit(solution)/shard_map/ppermute | solution.py:26
  (85 other events, 622.2 us)
Sparse Core Ops, SparseCore 0:
  9.7 20.1 all-gather.9
  31.5 30.7 all-gather.7
  63.9 37.4 all-gather.11
  102.8 37.4 all-gather.13
  141.7 37.4 all-gather.15
  521.0 24.8 reduce-scatter.7
  548.7 40.4 reduce-scatter.5
  591.7 47.8 reduce-scatter.13
  642.3 47.8 reduce-scatter.9
  692.5 47.8 reduce-scatter.11
where the time goes:
time: 1130 us; the launch traced here: 1120 us
  blocking collectives  406 us (36%)
  waiting for transfers between devices  332 us (29%)
  matrix products  188 us (17%)
  local copies, waits for them, and re-layouts  119 us (11%)
  other arithmetic  44.5 us (4%)
  between operations  17.8 us (2%)
    psum x1, blocking collectives, body(): totals = lax.psum(shard_sums, ('section', 'replica'))  371 us
    reduce_scatter x5, waiting for transfers between devices, body(): lax.psum_scatter(as_sent(all_sums), 'group', scatter_dimension=0, tiled=T...  167 us
    dot_general x8, matrix products, project(): return jnp.dot(left_side, right_side, preferred_element_type=jnp.float32)  61.6 us
    dot_general x8, matrix products, times_transpose(): lax.dot_general(left_side, right_side, (((1,), (1,)), ((), ())), preferre...  57.1 us
    ppermute x4, waiting for transfers between devices, from_behind(): return lax.ppermute(block, axis, route)  52.5 us
    dot_general x8, matrix products, contract_rows(): lax.dot_general(left_side, right_side, (((0,), (0,)), ((), ())), preferre...  52.2 us
    all_gather x1, waiting for transfers between devices, body(): lax.all_gather(ffn_in_weight, 'group', axis=0, tiled=True)  39.1 us
    all_gather x1, waiting for transfers between devices, body(): lax.all_gather(ffn_out_weight, 'group', axis=0, tiled=True)  38.9 us
  transfers between devices with their start and end apart: 16, of which 13 were waited for; matrix products, arithmetic and copies ran while one was open for 8% of the time, Pallas kernels for 0%

commit v1 on v0

--- a/solution.py
+++ b/solution.py
@@ -1,6 +1,8 @@
 import jax
 import jax.numpy as jnp
 from jax import lax
+from jax.experimental import pallas as pl
+from jax.experimental.pallas import tpu as pltpu
 from jax.sharding import PartitionSpec as P
 
 D = 768
@@ -9,29 +11,10 @@
 FF = 3072
 WIN = 128
 KERNEL = 4
-MB = 2
 
 
 norm_eps = 1e-06
 mask_value = -10000.0
-
-
-def from_behind(block, axis, distance):
-    devices = range(lax.axis_size(axis))
-    route = [(i - distance, i) for i in devices if i - distance in devices]
-    return lax.ppermute(block, axis, route)
-
-
-def swapped(array, axis, distance):
-    return lax.ppermute(array, axis, [(i, i ^ 1 << distance) for i in range(lax.axis_size(axis))])
-
-
-def as_sent(array):
-
-    def short(part):
-        return part.astype(jnp.bfloat16) if part.dtype == jnp.float32 else part
-
-    return jax.tree.map(short, array)
 
 
 def layer_norm(values, norm_gain, norm_shift):
@@ -77,24 +60,6 @@
         "wqhd,wkhd->whqk", queries, keys_all, preferred_element_type=jnp.float32
     )
     return raw_scores * HEAD_DIM ** (-0.5) + key_bias
-
-
-def rows_of(array, index, count):
-    return array[index * count : (index + 1) * count]
-
-
-def kept_zeros(row_count):
-    windows = row_count // WIN
-    return (
-        jnp.zeros((row_count, D), jnp.bfloat16),
-        jnp.zeros((row_count, 3 * D), jnp.bfloat16),
-        jnp.zeros((windows, HEADS, WIN, 1), jnp.float32),
-        jnp.zeros((row_count, D), jnp.bfloat16),
-        jnp.zeros((row_count, D), jnp.float32),
-        jnp.zeros((row_count, D), jnp.bfloat16),
-        jnp.zeros((row_count, FF), jnp.float32),
-        jnp.zeros((row_count, FF), jnp.bfloat16),
-    )
 
 
 def first_forward(weights, row_chars, row_codes):
@@ -259,6 +224,476 @@
     )
 
 
+MESH = pl.DeviceIdType.MESH
+GROUPS = 4
+RING = 4
+SHARD = D // GROUPS
+PIECE = SHARD // RING
+WIDE = 512
+SIDE = D - WIDE
+HALF = SHARD // 2
+CHUNKS = (
+    [(0, "col", j) for j in range(3)]
+    + [(1, "col", 0)]
+    + [(2, "col", j) for j in range(4)]
+    + [(3, "row", j) for j in range(4)]
+    + [(4, "row", j) for j in range(4)]
+)
+COUNT = len(CHUNKS)
+FULL_SHAPES = [(D, 3 * D), (D, D), (D, FF), (FF, D), (KERNEL * D, D)]
+SHARD_SHAPES = [(rows // GROUPS, cols) for rows, cols in FULL_SHAPES]
+VEC = (16, 256)
+
+
+def at16(value):
+    return pl.multiple_of(value, 16)
+
+
+def whole_block(refs, chunk, shard, first, rows):
+    mat, kind, j = CHUNKS[chunk]
+    if kind == "col":
+        return refs[mat].at[pl.ds(at16(shard * SHARD + first), rows), pl.ds(j * D, D)]
+    return refs[mat].at[pl.ds(at16(shard * D + j * SHARD + first), rows), :]
+
+
+def shard_block(refs, chunk, first, rows, col=0, cols=D):
+    mat, kind, j = CHUNKS[chunk]
+    if kind == "col":
+        return refs[mat].at[pl.ds(at16(first), rows), pl.ds(j * D + col, cols)]
+    return refs[mat].at[pl.ds(at16(j * SHARD + first), rows), pl.ds(col, cols)]
+
+
+def places():
+    s, g, r = lax.axis_index("section"), lax.axis_index("group"), lax.axis_index("replica")
+    near = {
+        "c": (s, g ^ 1, r),
+        "y": (s, g ^ 2, r),
+        "x": (1 - s, g, r),
+        "z1": (s, g, r ^ 1),
+        "z3": (s, g, r ^ 3),
+    }
+    return s, g, r, near
+
+
+def greet(targets):
+    barrier = pltpu.get_barrier_semaphore()
+    for target in targets:
+        pl.semaphore_signal(barrier, inc=1, device_id=target, device_id_type=MESH)
+    pl.semaphore_wait(barrier, len(targets))
+
+
+def remote(src, dst, send, recv, target):
+    return pltpu.make_async_remote_copy(
+        src_ref=src,
+        dst_ref=dst,
+        send_sem=send,
+        recv_sem=recv,
+        device_id=target,
+        device_id_type=MESH,
+    )
+
+
+def gather_kernel(*refs):
+    shards, vec, full, vecs = refs[:5], refs[5], refs[6:11], refs[11]
+    send, recv, own, vec_send, vec_recv = refs[12:]
+    s, g, r, near = places()
+    greet(list(near.values()) + [(s, g ^ 3, r)])
+    kinds = ("y", "x", "z1", "z3")
+    mine = lax.rem(r + 2 * s, RING)
+    piece = {
+        "y": mine,
+        "x": lax.rem(mine + 2, RING),
+        "z1": lax.rem((r ^ 1) + 2 * s, RING),
+        "z3": lax.rem((r ^ 3) + 2 * s, RING),
+    }
+    other = g ^ 2
+    started = []
+
+    def go(copy):
+        copy.start()
+        started.append(copy)
+
+    def block(chunk, shard, p):
+        return whole_block(full, chunk, shard, p * PIECE, PIECE)
+
+    for k in range(COUNT):
+        go(
+            remote(
+                shard_block(shards, k, mine * PIECE, PIECE),
+                block(k, g, mine),
+                send.at[0, k],
+                recv.at[0, k],
+                near["y"],
+            )
+        )
+    vec_copies = [
+        remote(vec, vecs.at[g], vec_send.at[i], vec_recv.at[i], (s, g ^ i, r)) for i in (1, 2, 3)
+    ]
+    for copy in vec_copies:
+        go(copy)
+    locals_ = [pltpu.make_async_copy(vec, vecs.at[g], vec_send.at[0])]
+    locals_[0].start()
+    for k in range(COUNT):
+        copy = pltpu.make_async_copy(
+            shard_block(shards, k, 0, SHARD), whole_block(full, k, g, 0, SHARD), own.at[k]
+        )
+        copy.start()
+        locals_.append(copy)
+        go(
+            remote(
+                shard_block(shards, k, 0, SHARD),
+                whole_block(full, k, g, 0, SHARD),
+                send.at[4, k],
+                recv.at[4, k],
+                near["c"],
+            )
+        )
+
+    def arrived(i, k):
+        p = piece[kinds[i]]
+        here = block(k, other, p)
+        remote(here, here, send.at[i, k], recv.at[i, k], near[kinds[i]]).wait_recv()
+        return here
+
+    for k in range(COUNT + 1):
+        if k < COUNT:
+            here = arrived(0, k)
+            for i in (1, 2, 3):
+                go(remote(here, here, send.at[i, k], recv.at[i, k], near[kinds[i]]))
+            remote(here, here, send.at[5, k], recv.at[5, k], near["c"]).start()
+        if k >= 1:
+            for i in (1, 2, 3):
+                here = arrived(i, k - 1)
+                remote(here, here, send.at[5, k - 1], recv.at[5, k - 1], near["c"]).start()
+    for copy in started:
+        copy.wait_send()
+    for k in range(COUNT):
+        theirs = whole_block(full, k, g ^ 1, 0, SHARD)
+        remote(theirs, theirs, send.at[4, k], recv.at[4, k], near["c"]).wait_recv()
+        sent = whole_block(full, k, other, 0, SHARD)
+        remote(sent, sent, send.at[5, k], recv.at[5, k], near["c"]).wait_send()
+        theirs = whole_block(full, k, g ^ 3, 0, SHARD)
+        remote(theirs, theirs, send.at[5, k], recv.at[5, k], near["c"]).wait_recv()
+    for copy in vec_copies:
+        copy.wait_recv()
+    for copy in locals_:
+        copy.wait()
+
+
+def gather_weights(shards, vec):
+    anywhere = pl.BlockSpec(memory_space=pl.ANY)
+    dma = pltpu.SemaphoreType.DMA
+    out = pl.pallas_call(
+        gather_kernel,
+        name="gather_weights",
+        out_shape=[jax.ShapeDtypeStruct(shape, jnp.bfloat16) for shape in FULL_SHAPES]
+        + [jax.ShapeDtypeStruct((GROUPS,) + VEC, jnp.bfloat16)],
+        in_specs=[anywhere] * 6,
+        out_specs=[anywhere] * 6,
+        scratch_shapes=[dma((6, COUNT)), dma((6, COUNT)), dma((COUNT,)), dma((4,)), dma((4,))],
+        compiler_params=pltpu.CompilerParams(collective_id=0, has_side_effects=True),
+    )(*shards, vec)
+    return out[:5], out[5]
+
+
+def add_into(dst, row, rows, col, cols, src, src_row=0):
+    @pl.loop(0, rows // 16)
+    def _(i):
+        here = pl.ds(at16(row + i * 16), 16)
+        there = pl.ds(at16(src_row + i * 16), 16)
+        columns = pl.ds(pl.multiple_of(col, 128), cols)
+        dst[here, columns] = dst[here, columns] + src[there, :]
+
+
+STAGES = 8
+
+
+def reduce_kernel(extra, *refs):
+    grads, vec, out, vec_out = refs[:5], refs[5], refs[6:11], refs[11]
+    (held, core_in, y_in, z1_in, z3_in, x_in, e3_in, e1_in, ex_in, ey_in, more_in) = refs[12:23]
+    vec_held, vec_in = refs[23:25]
+    (load, send, recv, more_send, more_recv, more_free, done, vec_send, vec_recv) = refs[25:]
+    s, g, r, near = places()
+    far = [(s, g, r ^ (RING << i)) for i in range(extra)]
+    greet(list(near.values()) + far)
+    y, c = g // 2, lax.rem(g, 2)
+    bit0, bit1 = lax.rem(r, 2), lax.rem(r // 2, 2)
+    first = lax.rem(bit0 + bit1, 2)
+    second = bit1
+    side_first, side_second = bit1, bit0
+    mine, other = 2 * y + c, 2 * (1 - y) + c
+
+    def spot(k, q):
+        return pl.multiple_of(k * D + q * SHARD, 16)
+
+    loads = {}
+    for k in range(COUNT):
+        loads[k] = []
+        for q in range(GROUPS):
+            copy = pltpu.make_async_copy(
+                whole_block(grads, k, q, 0, SHARD),
+                held.at[pl.ds(k * D + q * SHARD, SHARD)],
+                load.at[k, q],
+            )
+            copy.start()
+            loads[k].append(copy)
+
+    started = []
+
+    def go(k, i, src, dst, way):
+        copy = remote(src, dst, send.at[i, k], recv.at[i, k], near[way])
+        copy.start()
+        started.append(copy)
+        return copy
+
+    flight = {}
+
+    def cut(k, q, row, rows, col, cols):
+        return held.at[pl.ds(at16(spot(k, q) + row), rows), pl.ds(pl.multiple_of(col, 128), cols)]
+
+    b_row1 = first * HALF
+    b_row2 = b_row1 + second * PIECE
+    b_col = s * (WIDE // 2)
+    e_row1 = side_first * HALF
+    e_row2 = e_row1 + side_second * PIECE
+    e_col = WIDE + s * (SIDE // 2)
+
+    def final(k, row, rows, col, cols):
+        return shard_block(out, k, row, rows, pl.multiple_of(col, 128), cols)
+
+    def stage(n, k):
+        if n == 0:
+            for copy in loads[k]:
+                copy.wait()
+            flight[k] = [
+                go(
+                    k,
+                    i,
+                    held.at[pl.ds(spot(k, 2 * i + 1 - c), SHARD)],
+                    core_in.at[k, i],
+                    "c",
+                )
+                for i in range(2)
+            ]
+            return
+        for copy in flight[k]:
+            copy.wait_recv()
+        if n == 1:
+            for i in range(2):
+                add_into(held, spot(k, 2 * i + c), SHARD, 0, D, core_in.at[k, i])
+            flight[k] = [
+                go(k, 2, cut(k, other, 0, SHARD, 0, WIDE), y_in.at[k], "y"),
+                go(k, 3, cut(k, c, (1 - side_first) * HALF, HALF, WIDE, SIDE), e3_in.at[k, 0], "z3"),
+                go(
+                    k,
+                    4,
+                    cut(k, 2 + c, (1 - side_first) * HALF, HALF, WIDE, SIDE),
+                    e3_in.at[k, 1],
+                    "z3",
+                ),
+            ]
+        if n == 2:
+            add_into(held, spot(k, mine), SHARD, 0, WIDE, y_in.at[k])
+            send_row = (1 - first) * HALF
+            flight[k] = [go(k, 5, cut(k, mine, send_row, HALF, 0, WIDE), z1_in.at[k], "z1")]
+            for i in range(2):
+                add_into(held, spot(k, 2 * i + c) + e_row1, HALF, WIDE, SIDE, e3_in.at[k, i])
+                flight[k].append(
+                    go(
+                        k,
+                        6 + i,
+                        cut(k, 2 * i + c, e_row1 + (1 - side_second) * PIECE, PIECE, WIDE, SIDE),
+                        e1_in.at[k, i],
+                        "z1",
+                    )
+                )
+        if n == 3:
+            add_into(held, spot(k, mine) + b_row1, HALF, 0, WIDE, z1_in.at[k])
+            send_row = b_row1 + (1 - second) * PIECE
+            flight[k] = [go(k, 8, cut(k, mine, send_row, PIECE, 0, WIDE), z3_in.at[k], "z3")]
+            for i in range(2):
+                add_into(held, spot(k, 2 * i + c) + e_row2, PIECE, WIDE, SIDE, e1_in.at[k, i])
+                flight[k].append(
+                    go(
+                        k,
+                        9 + i,
+                        cut(k, 2 * i + c, e_row2, PIECE, WIDE + (1 - s) * (SIDE // 2), SIDE // 2),
+                        ex_in.at[k, i],
+                        "x",
+                    )
+                )
+        if n == 4:
+            add_into(held, spot(k, mine) + b_row2, PIECE, 0, WIDE, z3_in.at[k])
+            flight[k] = [
+                go(
+                    k,
+                    11,
+                    cut(k, mine, b_row2, PIECE, (1 - s) * (WIDE // 2), WIDE // 2),
+                    x_in.at[k],
+                    "x",
+                )
+            ]
+            for i in range(2):
+                add_into(
+                    held, spot(k, 2 * i + c) + e_row2, PIECE, e_col, SIDE // 2, ex_in.at[k, i]
+                )
+            flight[k].append(
+                go(k, 12, cut(k, other, e_row2, PIECE, e_col, SIDE // 2), ey_in.at[k], "y")
+            )
+        if n == 5:
+            add_into(held, spot(k, mine) + b_row2, PIECE, b_col, WIDE // 2, x_in.at[k])
+            add_into(held, spot(k, mine) + e_row2, PIECE, e_col, SIDE // 2, ey_in.at[k])
+            for i in range(extra):
+                for part, (row, col, cols) in enumerate(
+                    ((b_row2, b_col, WIDE // 2), (e_row2, e_col, SIDE // 2))
+                ):
+                    there = more_in.at[k, i, :, pl.ds(part * (WIDE // 2), cols)]
+                    copy = remote(
+                        cut(k, mine, row, PIECE, col, cols),
+                        there,
+                        more_send.at[part],
+                        more_recv.at[k, i, part],
+                        far[i],
+                    )
+                    copy.start()
+                    copy.wait()
+                    add_into(held, spot(k, mine) + row, PIECE, col, cols, there)
+            b_now, e_now = (
+                cut(k, mine, b_row2, PIECE, b_col, WIDE // 2),
+                cut(k, mine, e_row2, PIECE, e_col, SIDE // 2),
+            )
+            b_there = final(k, b_row2, PIECE, b_col, WIDE // 2)
+            e_there = final(k, e_row2, PIECE, e_col, SIDE // 2)
+            flight[k] = [go(k, 13, b_now, b_there, "z3"), go(k, 14, e_now, e_there, "z1")]
+            for i, (now, there) in enumerate(((b_now, b_there), (e_now, e_there))):
+                copy = pltpu.make_async_copy(now, there, done.at[i, k])
+                copy.start()
+                flight[k, i] = copy
+        if n == 6:
+            for i in range(2):
+                flight[k, i].wait()
+            b_now = final(k, b_row1, HALF, b_col, WIDE // 2)
+            e_now = final(k, e_row1, HALF, e_col, SIDE // 2)
+            flight[k] = [go(k, 15, b_now, b_now, "z1"), go(k, 16, e_now, e_now, "z3")]
+        if n == 7:
+            b_now = final(k, 0, SHARD, b_col, WIDE // 2)
+            e_now = final(k, 0, SHARD, e_col, SIDE // 2)
+            flight[k] = [go(k, 17, b_now, b_now, "x"), go(k, 18, e_now, e_now, "x")]
+
+    vec_load = pltpu.make_async_copy(vec, vec_held, vec_send.at[0])
+    vec_load.start()
+    vec_load.wait()
+    vec_copies = [
+        remote(
+            vec_held.at[2 * i + 1 - c],
+            vec_in.at[i],
+            vec_send.at[1 + i],
+            vec_recv.at[i],
+            near["c"],
+        )
+        for i in range(2)
+    ]
+    for copy in vec_copies:
+        copy.start()
+
+    def vec_stage(n):
+        if n == 0:
+            for i in range(2):
+                vec_copies[i].wait()
+                vec_held[2 * i + c] = vec_held[2 * i + c] + vec_in[i]
+            src = vec_held.at[other]
+        else:
+            vec_copies[-1].wait()
+            vec_held[mine] = vec_held[mine] + vec_in[1 + n]
+            src = vec_held.at[mine]
+        ways = [near["y"], near["z1"], near["z3"], near["x"]] + far
+        if n < len(ways):
+            copy = remote(src, vec_in.at[2 + n], vec_send.at[3 + n], vec_recv.at[2 + n], ways[n])
+            copy.start()
+            vec_copies.append(copy)
+        else:
+            copy = pltpu.make_async_copy(vec_held.at[mine], vec_out, vec_send.at[0])
+            copy.start()
+            copy.wait()
+
+    vec_steps = 5 + extra
+    for i in range(COUNT + STAGES - 1):
+        for n in reversed(range(STAGES)):
+            k = i - n
+            if 0 <= k < COUNT:
+                stage(n, k)
+        if 2 <= i < 2 + vec_steps:
+            vec_stage(i - 2)
+    for k in range(COUNT):
+        for copy in flight[k]:
+            copy.wait_recv()
+    for copy in started:
+        copy.wait_send()
+
+
+def reduce_grads(grads, vec, extra):
+    anywhere = pl.BlockSpec(memory_space=pl.ANY)
+    dma = pltpu.SemaphoreType.DMA
+    low = jnp.bfloat16
+    vmem = pltpu.VMEM
+    out = pl.pallas_call(
+        lambda *refs: reduce_kernel(extra, *refs),
+        name="reduce_grads",
+        out_shape=[jax.ShapeDtypeStruct(shape, low) for shape in SHARD_SHAPES]
+        + [jax.ShapeDtypeStruct(VEC, jnp.float32)],
+        in_specs=[anywhere] * 6,
+        out_specs=[anywhere] * 6,
+        scratch_shapes=[
+            vmem((COUNT * D, D), low),
+            vmem((COUNT, 2, SHARD, D), low),
+            vmem((COUNT, SHARD, WIDE), low),
+            vmem((COUNT, HALF, WIDE), low),
+            vmem((COUNT, PIECE, WIDE), low),
+            vmem((COUNT, PIECE, WIDE // 2), low),
+            vmem((COUNT, 2, HALF, SIDE), low),
+            vmem((COUNT, 2, PIECE, SIDE), low),
+            vmem((COUNT, 2, PIECE, SIDE // 2), low),
+            vmem((COUNT, PIECE, SIDE // 2), low),
+            vmem((COUNT, max(extra, 1), PIECE, D // 2), low),
+            vmem((GROUPS,) + VEC, jnp.float32),
+            vmem((6 + extra,) + VEC, jnp.float32),
+            dma((COUNT, GROUPS)),
+            dma((19, COUNT)),
+            dma((19, COUNT)),
+            dma((2,)),
+            dma((COUNT, max(extra, 1), 2)),
+            pltpu.SemaphoreType.REGULAR,
+            dma((2, COUNT)),
+            dma((7 + extra,)),
+            dma((6 + extra,)),
+        ],
+        compiler_params=pltpu.CompilerParams(
+            collective_id=1, has_side_effects=True, vmem_limit_bytes=56 << 20
+        ),
+    )(*grads, vec)
+    return out[:5], out[5]
+
+
+VEC_WIDTHS = [D, D, 2 * D, D, D, D, FF, D, D, D, D]
+
+
+def pack_vectors(vectors, lead):
+    rows = [v.reshape(lead + (-1, SHARD)) for v in vectors]
+    stacked = jnp.concatenate(rows, axis=-2)
+    pad = [(0, 0)] * len(lead) + [(0, VEC[0] - stacked.shape[-2]), (0, VEC[1] - SHARD)]
+    return jnp.pad(stacked, pad)
+
+
+def unpack_vectors(block):
+    parts = []
+    row = 0
+    for width in VEC_WIDTHS:
+        count = width // D
+        parts.append(block[..., row : row + count, :SHARD].reshape(-1))
+        row += count
+    return parts
+
+
 def body(
     chars,
     char_codes,
@@ -280,103 +715,67 @@
     down_norm_gain,
     down_norm_bias,
 ):
+    section = lax.axis_index("section")
+    vectors = [
+        attn_norm_gain,
+        attn_norm_bias,
+        qv_bias,
+        out_bias,
+        ffn_norm_gain,
+        ffn_norm_bias,
+        ffn_in_bias,
+        ffn_out_bias,
+        conv_bias,
+        down_norm_gain,
+        down_norm_bias,
+    ]
+    (qkv, outw, ffin, ffout, conv), vecs = gather_weights(
+        [qkv_weight, out_weight, ffn_in_weight, ffn_out_weight, conv_weight],
+        pack_vectors(vectors, ()),
+    )
+    (an_g, an_b, qv, ob, fn_g, fn_b, fib, fob, cb, dn_g, dn_b) = unpack_vectors(vecs)
     weights = (
-        lax.all_gather(attn_norm_gain, "group", axis=0, tiled=True),
-        lax.all_gather(attn_norm_bias, "group", axis=0, tiled=True),
-        lax.all_gather(qkv_weight, "group", axis=0, tiled=True),
-        lax.all_gather(qv_bias, "group", axis=0, tiled=True),
-        lax.all_gather(out_weight, "group", axis=0, tiled=True),
-        lax.all_gather(out_bias, "group", axis=0, tiled=True),
-        lax.all_gather(ffn_norm_gain, "group", axis=0, tiled=True),
-        lax.all_gather(ffn_norm_bias, "group", axis=0, tiled=True),
-        lax.all_gather(ffn_in_weight, "group", axis=0, tiled=True),
-        lax.all_gather(ffn_in_bias, "group", axis=0, tiled=True),
-        lax.all_gather(ffn_out_weight, "group", axis=0, tiled=True),
-        lax.all_gather(ffn_out_bias, "group", axis=0, tiled=True),
-        lax.all_gather(conv_weight, "group", axis=0, tiled=True),
-        lax.all_gather(conv_bias, "group", axis=0, tiled=True),
-        lax.all_gather(down_norm_gain, "group", axis=0, tiled=True),
-        lax.all_gather(down_norm_bias, "group", axis=0, tiled=True),
-    )
-    first_sums = tuple((jnp.zeros(weight.shape, jnp.float32) for weight in weights[:12]))
-    last_sums = tuple((jnp.zeros(weight.shape, jnp.float32) for weight in weights[12:]))
-    is_first = lax.axis_index("section") == 0
-    half_width = D // 2
-    mb_rows = chars.shape[0] // MB
-    mol_rows = mb_rows // KERNEL
-    inbound = jnp.zeros((mb_rows, D), jnp.bfloat16)
-    kept_store = []
-    grad_pieces = []
-    mol_pieces = []
-    for tick_index in range(MB + 2):
-        forward_index = tick_index if tick_index < MB else -1
-        back_index = tick_index - 2
-        down_index = tick_index - 1 if tick_index <= MB else -1
-
-        def first_section():
-            outbound = jnp.zeros((mb_rows, D), jnp.bfloat16)
-            kept_new = None
-            grad_rows = None
-            updated = first_sums
-            if forward_index >= 0:
-                outbound, kept_new = first_forward(
-                    weights,
-                    rows_of(chars, forward_index, mb_rows),
-                    rows_of(char_codes, forward_index, mb_rows),
-                )
-            if back_index >= 0:
-                grad_rows, increments = first_backward(
-                    weights,
-                    rows_of(chars, back_index, mb_rows),
-                    rows_of(char_codes, back_index, mb_rows),
-                    kept_store[back_index],
-                    inbound,
-                )
-                updated = jax.tree.map(jnp.add, updated, increments)
-            mol_new = jnp.zeros((mol_rows, D), jnp.bfloat16) if down_index >= 0 else None
-            return (outbound, updated, last_sums, kept_new, grad_rows, mol_new)
-
-        def last_section():
-            outbound = jnp.zeros((mb_rows, D), jnp.bfloat16)
-            updated = last_sums
-            mol_new = None
-            if down_index >= 0:
-                mol_new, outbound, increments = second_layer(
-                    weights, inbound, rows_of(mol_cotangent, down_index, mol_rows)
-                )
-                updated = jax.tree.map(jnp.add, updated, increments)
-            kept_new = kept_zeros(mb_rows) if forward_index >= 0 else None
-            grad_rows = jnp.zeros((mb_rows, D), jnp.float32) if back_index >= 0 else None
-            return (outbound, first_sums, updated, kept_new, grad_rows, mol_new)
-
-        outbound, first_sums, last_sums, kept_new, grad_rows, mol_new = lax.cond(
-            is_first, first_section, last_section
+        an_g, an_b, qkv, qv, outw, ob, fn_g, fn_b, ffin, fib, ffout, fob, conv, cb, dn_g, dn_b,
+    )
+    rows = chars.shape[0] // 2
+    mols = rows // KERNEL
+    my_chars = lax.dynamic_slice_in_dim(chars, section * rows, rows, 0)
+    my_codes = lax.dynamic_slice_in_dim(char_codes, section * rows, rows, 0)
+    my_cot = lax.dynamic_slice_in_dim(mol_cotangent, section * mols, mols, 0)
+    layer_out, kept = first_forward(weights, my_chars, my_codes)
+    mol, grad_handed, last = second_layer(weights, layer_out, my_cot)
+    grad_chars, first = first_backward(weights, my_chars, my_codes, kept, grad_handed)
+    half = D // 2
+
+    def meet(whole):
+        keep = lax.dynamic_slice_in_dim(whole, section * half, half, 1)
+        give = lax.dynamic_slice_in_dim(whole, (1 - section) * half, half, 1)
+        got = lax.ppermute(give, "section", [(0, 1), (1, 0)])
+        return jnp.where(
+            section == 0,
+            jnp.concatenate([keep, got], axis=0),
+            jnp.concatenate([got, keep], axis=0),
         )
-        if forward_index >= 0:
-            kept_store.append(kept_new)
-        if back_index >= 0:
-            grad_pieces.append(grad_rows)
-        if down_index >= 0:
-            mol_pieces.append(mol_new)
-        if tick_index <= MB:
-            empty_rows = jnp.zeros((mb_rows, D), jnp.bfloat16)
-            from_below = from_behind(outbound, "section", 1) if tick_index < MB else empty_rows
-            from_above = from_behind(outbound, "section", -1) if tick_index >= 1 else empty_rows
-            inbound = jnp.where(is_first, from_above, from_below)
-    grad_whole = jnp.concatenate(grad_pieces, axis=0).astype(jnp.bfloat16)
-    mol_whole = jnp.concatenate(mol_pieces, axis=0)
-    other_grad, other_mol = swapped(
-        (grad_whole[:, half_width:], mol_whole[:, :half_width]), "section", 0
-    )
-    chars_grad = jnp.where(is_first, grad_whole[:, :half_width], other_grad)
-    molecules = jnp.where(is_first, other_mol, mol_whole[:, half_width:])
-    all_sums = first_sums + last_sums
-    shard_sums = jax.tree.map(
-        lambda part: part.astype(jnp.float32),
-        lax.psum_scatter(as_sent(all_sums), "group", scatter_dimension=0, tiled=True),
-    )
-    totals = lax.psum(shard_sums, ("section", "replica"))
-    return (molecules, chars_grad) + tuple(totals)
+
+    molecules = meet(mol)
+    chars_grad = meet(grad_chars.astype(jnp.bfloat16))
+    g_an_g, g_an_b, g_qkv, g_qv, g_out, g_ob, g_fn_g, g_fn_b, g_in, g_fib, g_ffo, g_fob = first
+    g_conv, g_cb, g_dn_g, g_dn_b = last
+    vec_grads = [g_an_g, g_an_b, g_qv, g_ob, g_fn_g, g_fn_b, g_fib, g_fob, g_cb, g_dn_g, g_dn_b]
+    packed = pack_vectors([v.reshape(GROUPS, -1) for v in vec_grads], (GROUPS,))
+    sums, vec_sum = reduce_grads(
+        [w.astype(jnp.bfloat16) for w in (g_qkv, g_out, g_in, g_ffo, g_conv)],
+        packed,
+        (lax.axis_size("replica") // RING).bit_length() - 1,
+    )
+    t_qkv, t_out, t_in, t_ffo, t_conv = [w.astype(jnp.float32) for w in sums]
+    v = unpack_vectors(vec_sum)
+    return (
+        molecules,
+        chars_grad,
+        v[0], v[1], t_qkv, v[2], t_out, v[3], v[4], v[5], t_in, v[6], t_ffo, v[7], t_conv,
+        v[8], v[9], v[10],
+    )
 
 
 def solution(mesh):

time: 1130 us -> 524 us (0.46)
  blocking collectives: 406 us -> 0 us
  Pallas kernels: 0 us -> 332 us
  waiting for transfers between devices: 332 us -> 0.01 us
  matrix products: 188 us -> 96.8 us
  local copies, waits for them, and re-layouts: 119 us -> 50.1 us
  between operations: 17.8 us -> 1.88 us
  other arithmetic: 44.5 us -> 31.8 us
    psum x1 -> x0, blocking collectives: 371 us -> none  [body(): totals = lax.psum(shard_sums, ('section', 'replica'))]
    pallas_call x0 -> x2, Pallas kernels: none -> 332 us  [the longest x1 181 us: reduce_grads(): pl.pallas_call(lambda *refs: reduce_kernel(extra, *refs), name='reduce_gr...]
    reduce_scatter x5 -> x0, waiting for transfers between devices: 167 us -> none  [body(): lax.psum_scatter(as_sent(all_sums), 'group', scatter_dimension=0, tiled=T...]
    all_gather x5 -> x0, waiting for transfers between devices: 102 us -> none  [the longest x1 39.1 us: body(): lax.all_gather(ffn_in_weight, 'group', axis=0, tiled=True)]
    ppermute x6 -> x2, waiting for transfers between devices: 59.7 us -> 0.01 us  [meet(): got = lax.ppermute(give, 'section', [(0, 1), (1, 0)])]
    cond x136 -> x0, local copies, waits for them, and re-layouts: 34.7 us -> none  [the longest x4 26.7 us: body(): lax.cond(is_first, first_section, last_section)]
    dot_general x8 -> x5, matrix products: 52.2 us -> 18.9 us  [contract_rows(): lax.dot_general(left_side, right_side, (((0,), (0,)), ((), ())), preferre...]
    dot_general x8 -> x5, matrix products: 57.1 us -> 27.8 us  [times_transpose(): lax.dot_general(left_side, right_side, (((1,), (1,)), ((), ())), preferre...]
  transfers between devices with their start and end apart: 16 -> 2, of which waited for: 13 -> 0; matrix products, arithmetic and copies ran while one was open for 8% -> 7% of each run, Pallas kernels for 0% -> 35%
where the time goes in v1:
time: 524 us; the launch traced here: 515 us
  Pallas kernels  332 us (63%)
  matrix products  96.8 us (18%)
  local copies, waits for them, and re-layouts  50.1 us (10%)
  other arithmetic  31.8 us (6%)
    pallas_call x1, Pallas kernels, reduce_grads(): pl.pallas_call(lambda *refs: reduce_kernel(extra, *refs), name='reduce_gr...  181 us
    pallas_call x1, Pallas kernels, gather_weights(): pl.pallas_call(gather_kernel, name='gather_weights', out_shape=[jax.Shape...  151 us
    dot_general x5, matrix products, project(): return jnp.dot(left_side, right_side, preferred_element_type=jnp.float32)  39.8 us
    dot_general x5, matrix products, times_transpose(): lax.dot_general(left_side, right_side, (((1,), (1,)), ((), ())), preferre...  27.8 us
    dot_general x5, matrix products, contract_rows(): lax.dot_general(left_side, right_side, (((0,), (0,)), ((), ())), preferre...  18.9 us
  transfers between devices with their start and end apart: 2, of which 0 were waited for; matrix products, arithmetic and copies ran while one was open for 7% of the time, Pallas kernels for 35%

profile of v1, /device:TPU:0, one launch (start us, length us, event | category | flops | bytes accessed | tf_op | source)
XLA Modules:
  0.0 514.9 jit_solution(3388734810918089234)
XLA Ops:
  9.0 151.3 %gather_weights.1 = (bf16[768,2304]{1,0:T(8,128)(2,1)}, bf16[768,768]{1,0:T(8,128)(2,1)}, bf16[768,3072]{1,0:T(8,128)(2,1)}, bf16[3072,768]{1,0:T(8,128)(2,1)}, ...) custom-call(bf16[192,2304]{1,0:T(8,128)(2,1)} %refs_0_.1, bf16[192,768]{1,0:T(8,128)(2,1)} %refs_1_.1, ...), custom_call_target="tpu_custom_call" | custom-call | tf_op jit(solution)/shard_map/gather_weights/pallas_call | solution.py:386
  164.5 5.6 %fusion.6 = bf16[512,2304]{1,0:T(8,128)(2,1)} fusion(bf16[768,2304]{1,0:T(8,128)(2,1)} %get-tuple-element.31, f32[2304]{0:T(1024)S(1)} %maximum_convert_fusion.1, f32[768]{0:T(1024)S(1)} %reshape.369, f32[768]{0:T(1024)S(1)} %reshape.368, f32[512]{0:T(512)S(1)} %fusion.49, f32[512]{0:T(512)S(1)} %broadcast_multiply_fusion.1, ...), kind=kOutput, calls=%fused_computation.25 | convolution fusion | flops 1816657920 | bytes 6709252 | tf_op jit(solution)/shard_map/dot_general | solution.py:31
  170.1 4.3 copy.46
  174.4 4.2 reshape.353
  184.0 2.7 fusion.68
  188.5 20.8 %multiply_convert_fusion = (bf16[512,3072]{1,0:T(8,128)(2,1)S(1)}, f32[512,3072]{1,0:T(8,128)}, f32[512,3072]{1,0:T(8,128)}) fusion(f32[3072]{0:T(1024)S(1)} %reshape.373, bf16[768,3072]{1,0:T(8,128)(2,1)} %get-tuple-element.33, f32[512,768]{1,0:T(8,128)} %copy-done.10, f32[768]{0:T(1024)S(1)} %reshape.372, f32[768]{0:T(1024)S(1)} %reshape.371, ...), kind=kOutput, calls=%fused_computation.4 | convolution fusion | flops 2521694208 | bytes 22042624 | tf_op jit(solution)/shard_map/dot_general | solution.py:31
  211.0 5.8 %add_convert_fusion.2 = bf16[512,768]{1,0:T(8,128)(2,1)} fusion(f32[512,768]{1,0:T(8,128)S(1)} %copy-done.11, bf16[512,3072]{1,0:T(8,128)(2,1)S(1)} %get-tuple-element.76, bf16[3072,768]{1,0:T(8,128)(2,1)} %get-tuple-element.34, f32[768]{0:T(1024)S(1)} %reshape.374), kind=kOutput, calls=%fused_computation.64 | convolution fusion | flops 2417098752 | bytes 10226688 | tf_op jit(solution)/shard_map/dot_general | solution.py:31
  219.1 5.0 fusion.61
  230.7 2.9 convert_reduce_fusion.6
  234.3 4.9 convolution_convert_fusion.4
  239.1 2.7 reshape.355
  241.9 11.3 %convert_reduce_fusion = (f32[3072]{0:T(1024)}, bf16[512,3072]{1,0:T(8,128)(2,1)S(1)}) fusion(f32[512,3072]{1,0:T(8,128)} %get-tuple-element.77, f32[512,3072]{1,0:T(8,128)} %get-tuple-element.107, f32[3072]{0:T(1024)S(1)} %copy-done.57, bf16[512,768]{1,0:T(8,128)(2,1)} %reshape.355, bf16[3072,768]{1,0:T(8,128)(2,1)} %get-tuple-element.34), kind=kOutput, calls=%fused_computation.2 | convolution fusion | flops 2442654720 | bytes 21258240 | tf_op jit(solution)/shard_map/dot_general | solution.py:41
  253.2 7.0 %multiply_reduce_fusion.1 = (f32[768]{0:T(1024)}, f32[512]{0:T(512)S(1)}, f32[768]{0:T(1024)}, f32[512,768]{1,0:T(8,128)S(1)}) fusion(f32[512,768]{1,0:T(8,128)S(1)} %copy-done.12, f32[512]{0:T(512)S(1)} %copy-done.59, f32[512]{0:T(512)S(1)} %copy-done.36, f32[768]{0:T(1024)S(1)} %copy-done.52, bf16[512,3072]{1,0:T(8,128)(2,1)S(1)} %get-tuple-element.66, ...), kind=kOutput, calls=%fused_computation.58 | convolution fusion | flops 2419062784 | bytes 11025408 | tf_op jit(solution)/shard_map/dot_general | solution.py:41
  265.5 2.3 copy.52
  267.9 2.6 reshape.356
  270.5 2.7 multiply_reduce_fusion
  280.1 3.1 convert_reduce_fusion.1
  285.5 2.9 fusion.58
  296.9 3.8 convolution_convert_fusion.refs_4_
  300.7 4.4 convolution_convert_fusion.1.refs_3_
  305.2 4.9 convolution_convert_fusion.2.refs_2_
  312.0 4.1 convolution_convert_fusion.3.refs_0_
  317.9 180.9 %reduce_grads.1 = (bf16[192,2304]{1,0:T(8,128)(2,1)}, bf16[192,768]{1,0:T(8,128)(2,1)}, bf16[192,3072]{1,0:T(8,128)(2,1)}, bf16[768,768]{1,0:T(8,128)(2,1)}, bf1...) custom-call(bf16[768,2304]{1,0:T(8,128)(2,1)} %convolution_convert_fusion.3.refs_0_, ...), custom_call_target="tpu_custom_call" | custom-call | tf_op jit(solution)/shard_map/reduce_grads/pallas_call | solution.py:639
  501.8 3.0 convert_element_type.280
  (252 shorter events, 70.0 us)
Async XLA Ops:
  0.7 162.9 %copy-start.14 = (bf16[1024,768]{1,0:T(8,128)(2,1)S(1)}, bf16[1024,768]{1,0:T(8,128)(2,1)}, u32[]{:S(2)}) copy-start(bf16[1024,768]{1,0:T(8,128)(2,1)} %param.19) | copy-start | bytes 4718596
  164.1 5.9 %copy-start.37 = (f32[512]{0:T(512)}, f32[512]{0:T(512)S(1)}, u32[]{:S(2)}) copy-start(f32[512]{0:T(512)S(1)} %fusion.23) | copy-start | bytes 6148
  164.1 5.9 %copy-start.41 = (f32[512]{0:T(512)}, f32[512]{0:T(512)S(1)}, u32[]{:S(2)}) copy-start(f32[512]{0:T(512)S(1)} %fusion.49) | copy-start | bytes 6148
  186.7 22.6 %copy-start.35 = (f32[512]{0:T(512)}, f32[512]{0:T(512)S(1)}, u32[]{:S(2)}) copy-start(f32[512]{0:T(512)S(1)} %broadcast_multiply_fusion) | copy-start | bytes 6148
  188.1 21.2 %copy-start.39 = (f32[512]{0:T(512)}, f32[512]{0:T(512)S(1)}, u32[]{:S(2)}) copy-start(f32[512]{0:T(512)S(1)} %multiply_reduce_fusion.3) | copy-start | bytes 6148
  188.1 21.2 %copy-start.58 = (f32[512]{0:T(512)}, f32[512]{0:T(512)S(1)}, u32[]{:S(2)}) copy-start(f32[512]{0:T(512)S(1)} %fusion.50) | copy-start | bytes 6148
  188.2 21.1 %copy-start.51 = (f32[768]{0:T(1024)}, f32[768]{0:T(1024)S(1)}, u32[]{:S(2)}) copy-start(f32[768]{0:T(1024)S(1)} %reshape.371) | copy-start | bytes 9220
  188.3 21.0 %copy-start.65 = (f32[768]{0:T(1024)}, f32[768]{0:T(1024)S(1)}, u32[]{:S(2)}) copy-start(f32[768]{0:T(1024)S(1)} %reshape.372) | copy-start | bytes 9220
  188.4 20.9 %copy-start.56 = (f32[3072]{0:T(1024)}, f32[3072]{0:T(1024)S(1)}, u32[]{:S(2)}) copy-start(f32[3072]{0:T(1024)S(1)} %reshape.373) | copy-start | bytes 36868
  188.5 22.5 %copy-start.11 = (f32[512,768]{1,0:T(8,128)S(1)}, f32[512,768]{1,0:T(8,128)}, u32[]{:S(2)}) copy-start(f32[512,768]{1,0:T(8,128)} %copy-done.10) | copy-start | bytes 4718596
  234.3 7.5 %copy-start.57 = (f32[3072]{0:T(1024)S(1)}, f32[3072]{0:T(1024)}, u32[]{:S(2)}) copy-start(f32[3072]{0:T(1024)} %copy-done.56) | copy-start | bytes 36868
  241.8 11.4 %copy-start.12 = (f32[512,768]{1,0:T(8,128)S(1)}, f32[512,768]{1,0:T(8,128)}, u32[]{:S(2)}) copy-start(f32[512,768]{1,0:T(8,128)} %copy-done.10) | copy-start | bytes 4718596
  241.8 11.4 %copy-start.36 = (f32[512]{0:T(512)S(1)}, f32[512]{0:T(512)}, u32[]{:S(2)}) copy-start(f32[512]{0:T(512)} %copy-done.35) | copy-start | bytes 6148
  241.8 11.3 %copy-start.52 = (f32[768]{0:T(1024)S(1)}, f32[768]{0:T(1024)}, u32[]{:S(2)}) copy-start(f32[768]{0:T(1024)} %copy-done.51) | copy-start | bytes 9220
  241.8 11.3 %copy-start.59 = (f32[512]{0:T(512)S(1)}, f32[512]{0:T(512)}, u32[]{:S(2)}) copy-start(f32[512]{0:T(512)} %copy-done.58) | copy-start | bytes 6148
  253.2 7.1 %copy-start.73 = (bf16[512,3072]{1,0:T(8,128)(2,1)}, bf16[512,3072]{1,0:T(8,128)(2,1)S(1)}, u32[]{:S(2)}) copy-start(bf16[512,3072]{1,0:T(8,128)(2,1)S(1)} %get-tuple-element.66) | copy-start | bytes 9437188
  253.2 7.0 %copy-start.40 = (f32[512]{0:T(512)S(1)}, f32[512]{0:T(512)}, u32[]{:S(2)}) copy-start(f32[512]{0:T(512)} %copy-done.39) | copy-start | bytes 6148
  263.8 6.6 %copy-start.27 = (f32[4,12,128]{2,1,0:T(8,128)S(1)}, f32[4,12,128]{2,1,0:T(8,128)}, u32[]{:S(2)}) copy-start(f32[4,12,128]{2,1,0:T(8,128)} %copy-done.26) | copy-start | bytes 73732
  289.8 7.1 %copy-start.17 = (bf16[128,3072]{1,0:T(8,128)(2,1)S(1)}, bf16[128,3072]{1,0:T(8,128)(2,1)}, u32[]{:S(2)}) copy-start(bf16[128,3072]{1,0:T(8,128)(2,1)} %reshape.354) | copy-start | bytes 2359300
  289.8 7.1 %copy-start.21 = (bf16[128,768]{1,0:T(8,128)(2,1)S(1)}, bf16[128,768]{1,0:T(8,128)(2,1)}, u32[]{:S(2)}) copy-start(bf16[128,768]{1,0:T(8,128)(2,1)} %copy-done.20) | copy-start | bytes 589828
  294.2 218.0 %collective-permute-start.1 = (bf16[512,384]{1,0:T(8,128)(2,1)}, bf16[512,384]{1,0:T(8,128)(2,1)}, u32[]{:S(2)}, u32[]{:S(2)}) collective-permute-start(bf16[512,384]{1,0:T(8,128)(2,1)} %get-tuple-element.84), channel_id=1, source_target_pairs={{0,16},{16,0},{1,17},{17,1},{2,18},{18,2},{3,19},{19,3},{4,20},{20... | collective-permute-start | bytes 1179656 | tf_op jit(solution)/shard_map/ppermute | solution.py:753
  296.4 215.1 %collective-permute-start = (bf16[128,384]{1,0:T(8,128)(2,1)}, bf16[128,384]{1,0:T(8,128)(2,1)S(1)}, u32[]{:S(2)}, u32[]{:S(2)}) collective-permute-start(bf16[128,384]{1,0:T(8,128)(2,1)} %get-tuple-element.87), channel_id=1, source_target_pairs={{0,16},{16,0},{1,17},{17,1},{2,18},{18,2},{3,19},{19,3},{4,20},{20... | collective-permute-start | bytes 294920 | tf_op jit(solution)/shard_map/ppermute | solution.py:753
  305.2 6.7 %copy-start.19 = (bf16[4,128,3,12,64]{1,0,4,3,2:T(4,128)(2,1)S(1)}, bf16[4,128,3,12,64]{1,0,4,3,2:T(4,128)(2,1)}, u32[]{:S(2)}) copy-start(bf16[4,128,3,12,64]{1,0,4,3,2:T(4,128)(2,1)} %copy-done.18) | copy-start | bytes 7077892
  498.8 6.0 %copy-start.24 = (bf16[768,768]{1,0:T(8,128)(2,1)S(1)}, bf16[768,768]{1,0:T(8,128)(2,1)}, u32[]{:S(2)}) copy-start(bf16[768,768]{1,0:T(8,128)(2,1)} %get-tuple-element.40) | copy-start | bytes 3538948
  (55 other events, 183.3 us)

commit v2 on v0

v2 whole, which is shorter than its diff:
```python
import functools

import jax
import jax.numpy as jnp
from jax import lax
from jax.experimental import pallas as pl
from jax.experimental.pallas import tpu as pltpu
from jax.sharding import PartitionSpec as P

D = 768
HEADS = 12
HEAD_DIM = 64
FF = 3072
WIN = 128
KERNEL = 4
GROUPS = 4
RING = 4
SHARD = D // GROUPS
THIRD = SHARD // 3
HALF = D // 2
TILE = 256
PAIR = 2 * HEAD_DIM
PAIRS = HEADS // 2
RUN = WIN // KERNEL
BLOCKS = FF // D
VEC = (16, 256)
norm_eps = 1e-06
mask_value = -10000.0
MESH = pl.DeviceIdType.MESH
F32 = jnp.float32
LOW = jnp.bfloat16

CHUNKS = (
    [(0, "col", j) for j in range(3)]
    + [(1, "col", 0)]
    + [(2, "col", j) for j in range(4)]
    + [(3, "row", j) for j in range(4)]
    + [(4, "row", j) for j in range(4)]
)
COUNT = len(CHUNKS)
QKV, OUT, FIN, FOUT, CONV = BASES = (0, 3, 4, 8, 12)
SHARD_SHAPES = [(SHARD, 3 * D), (SHARD, D), (SHARD, FF), (FF // GROUPS, D), (D, D)]

A_GAIN, A_BIAS, Q_BIAS, V_BIAS, O_BIAS, F_GAIN, F_BIAS = range(7)
IN_BIAS, FO_BIAS, C_BIAS, D_GAIN, D_BIAS = 7, 11, 12, 13, 14


def segments():
    table = {}
    for row, at in zip((A_GAIN, A_BIAS, O_BIAS, F_GAIN, F_BIAS), (0, 1, 4, 5, 6)):
        table[row] = [(q, at) for q in range(GROUPS)]
    table[Q_BIAS] = [(0, 2), (0, 3), (1, 2), (1, 3)]
    table[V_BIAS] = [(2, 2), (2, 3), (3, 2), (3, 3)]
    for n in range(BLOCKS):
        table[IN_BIAS + n] = [(n, 7 + i) for i in range(4)]
    for row, at in zip((FO_BIAS, C_BIAS, D_GAIN, D_BIAS), (11, 12, 13, 14)):
        table[row] = [(q, at) for q in range(GROUPS)]
    return table


SEGMENTS = segments()


def at16(value):
    return pl.multiple_of(value, 16)


def at128(value):
    return pl.multiple_of(value, 128)


def spot(chunk, shard, first=0):
    mat, kind, j = CHUNKS[chunk]
    if kind == "col":
        return at16((BASES[mat] + j) * D + shard * SHARD + first)
    return at16((BASES[mat] + shard) * D + j * SHARD + first)


def shard_block(refs, chunk, first, rows, col=0, cols=D):
    mat, kind, j = CHUNKS[chunk]
    if kind == "col":
        return refs[mat].at[pl.ds(at16(first), rows), pl.ds(at128(j * D + col), cols)]
    return refs[mat].at[pl.ds(at16(j * SHARD + first), rows), pl.ds(at128(col), cols)]


def remote(src, dst, send, recv, target):
    return pltpu.make_async_remote_copy(
        src_ref=src,
        dst_ref=dst,
        send_sem=send,
        recv_sem=recv,
        device_id=target,
        device_id_type=MESH,
    )


def add_into(dst, row, rows, col, cols, src):
    @pl.loop(0, rows // 16)
    def _(i):
        here = pl.ds(at16(row + i * 16), 16)
        columns = pl.ds(at128(col), cols)
        dst[here, columns] = dst[here, columns] + src[pl.ds(at16(i * 16), 16), :]


def dot(left, right):
    return jnp.dot(left, right, preferred_element_type=F32)


def dot_rows(left, right):
    return lax.dot_general(left, right, (((0,), (0,)), ((), ())), preferred_element_type=F32)


def dot_turned(left, right):
    return lax.dot_general(left, right, (((1,), (1,)), ((), ())), preferred_element_type=F32)


def normalized(values):
    center = values - jnp.mean(values, axis=-1, keepdims=True)
    scale = lax.rsqrt(jnp.mean(center * center, axis=-1, keepdims=True) + norm_eps)
    return center * scale, scale


def norm_back(unit, scale, gain, grad):
    grad_unit = grad * gain
    mean_grad = jnp.mean(grad_unit, axis=-1, keepdims=True)
    mean_both = jnp.mean(grad_unit * unit, axis=-1, keepdims=True)
    return scale * (grad_unit - mean_grad - unit * mean_both)


def gelu_parts(values):
    half = 0.5 * lax.erf(values * (0.5**0.5)) + 0.5
    bell = jnp.exp(-0.5 * values * values) * 0.3989422804014327
    return values * half, half + values * bell


def column_sum(values):
    return jnp.sum(values, axis=0, keepdims=True)


def program_kernel(rows, extra, *refs):
    (chars, codes, cotangent, vec) = refs[:4]
    shards = refs[4:9]
    mols_out, chars_out, vec_out = refs[9:12]
    out = refs[12:17]
    more_in = refs[17] if extra else None
    refs = refs[:17] + refs[17 + (extra > 0) :]
    (
        held,
        core_in,
        y_in,
        x_in,
        e_in,
        m_in,
        vecs,
        vec_segs,
        rows_f32,
        vec_grads,
        vec_in,
        chars_v,
        cot_v,
        normed,
        projected,
        probs,
        context,
        hidden,
        normed_ffn,
        slope,
        active,
        layer,
        stacked,
        low_grad,
        total,
        mol_v,
    ) = refs[17:43]
    (
        w_send,
        w_recv,
        w_own,
        g_send,
        g_recv,
        g_own,
        more_send,
        more_recv,
        v_send,
        v_recv,
        io_sem,
        swap_send,
        swap_recv,
    ) = refs[43:]
    windows = rows // WIN
    mols = rows // KERNEL
    s, g, r = lax.axis_index("section"), lax.axis_index("group"), lax.axis_index("replica")
    near = {
        "c": (s, g ^ 1, r),
        "y": (s, g ^ 2, r),
        "x": (1 - s, g, r),
        "e": (s, g, r ^ 1),
        "m": (s, g, r ^ 3),
        "d": (s, g ^ 3, r),
        "w": (s, g, r ^ 2),
    }
    far = [(s, g, r ^ (RING << i)) for i in range(extra)]
    place = lax.rem(r, RING)
    even = lax.rem(r, 2) == 0
    middle = jnp.logical_or(place == 1, place == 2)
    border = jnp.logical_not(middle)

    loads = [
        pltpu.make_async_copy(chars.at[pl.ds(at16(s * rows), rows)], chars_v, io_sem.at[0]),
        pltpu.make_async_copy(cotangent.at[pl.ds(at16(s * mols), mols)], cot_v, io_sem.at[1]),
        pltpu.make_async_copy(vec, vecs.at[g], io_sem.at[2]),
    ]
    for copy in loads:
        copy.start()
    for k in range(COUNT):
        own_block = held.at[pl.ds(spot(k, g), SHARD)]
        pltpu.make_async_copy(shard_block(shards, k, 0, SHARD), own_block, w_own.at[k]).start()

    barrier = pltpu.get_barrier_semaphore()
    greeted = list(near.values()) + far
    for target in greeted:
        pl.semaphore_signal(barrier, inc=1, device_id=target, device_id_type=MESH)
    pl.semaphore_wait(barrier, len(greeted))

    y_third = jnp.where(even, s, 2)
    z_third = jnp.where(even, 2, s)
    x_third = 1 - s
    other = g ^ 2

    vec_copies = [
        remote(vec, vecs.at[g], v_send.at[i], v_recv.at[i], near[way])
        for i, way in enumerate("cyd")
    ]
    for copy in vec_copies:
        copy.start()

    def hop(i, k, third, way):
        here = held.at[pl.ds(spot(k, other, third * THIRD), THIRD)]
        return remote(here, here, w_send.at[i, k], w_recv.at[i, k], near[way])

    def first_hop(k):
        return remote(
            shard_block(shards, k, y_third * THIRD, THIRD),
            held.at[pl.ds(spot(k, g, y_third * THIRD), THIRD)],
            w_send.at[0, k],
            w_recv.at[0, k],
            near["y"],
        )

    def core_own(k):
        return remote(
            shard_block(shards, k, 0, SHARD),
            held.at[pl.ds(spot(k, g), SHARD)],
            w_send.at[3, k],
            w_recv.at[3, k],
            near["c"],
        )

    def core_hop(k, third):
        hop(4, k, third, "c").start()

    def core_wait(k):
        here = held.at[pl.ds(spot(k, other), SHARD)]
        return remote(here, here, w_send.at[4, k], w_recv.at[4, k], near["c"])

    for k in range(COUNT):
        first_hop(k).start()
    for k in range(COUNT):
        core_own(k).start()

    z_lag, x_lag = 2, 4

    def gather_step(k):
        if k < COUNT:
            hop(0, k, y_third, "y").wait_recv()
            hop(2, k, y_third, "e").start()

            @pl.when(even)
            def _():
                hop(1, k, s, "x").start()

            core_hop(k, y_third)
        j = k - z_lag
        if 0 <= j < COUNT:
            hop(2, j, z_third, "e").wait_recv()

            @pl.when(jnp.logical_not(even))
            def _():
                hop(1, j, s, "x").start()

            core_hop(j, z_third)
        j = k - x_lag
        if 0 <= j < COUNT:
            hop(1, j, x_third, "x").wait_recv()
            core_hop(j, x_third)

    def weight_ready(k):
        own_block = held.at[pl.ds(spot(k, g), SHARD)]
        pltpu.make_async_copy(shard_block(shards, k, 0, SHARD), own_block, w_own.at[k]).wait()
        theirs = held.at[pl.ds(spot(k, g ^ 1), SHARD)]
        remote(theirs, theirs, w_send.at[3, k], w_recv.at[3, k], near["c"]).wait_recv()
        theirs = held.at[pl.ds(spot(k, g ^ 3), SHARD)]
        remote(theirs, theirs, w_send.at[4, k], w_recv.at[4, k], near["c"]).wait_recv()

    def gather_done():
        for k in range(COUNT):
            first_hop(k).wait_send()
            hop(2, k, y_third, "e").wait_send()
            hop(1, k, s, "x").wait_send()
            core_own(k).wait_send()
            core_wait(k).wait_send()

    def spread_matrix(seg):
        i = lax.broadcasted_iota(jnp.int32, (VEC[1], D), 0)
        j = lax.broadcasted_iota(jnp.int32, (VEC[1], D), 1)
        hit = jnp.logical_and(j == i + seg * SHARD, i < SHARD)
        return jnp.where(hit, 1.0, 0.0).astype(LOW)

    def vectors_ready():
        loads[2].wait()
        for copy in vec_copies:
            copy.wait()
        vec_segs[...] = jnp.zeros_like(vec_segs)
        for row, parts in SEGMENTS.items():
            for seg, (q, at) in enumerate(parts):
                vec_segs[seg, row : row + 1, :] = vecs[q, at : at + 1, :]
        full = jnp.zeros((VEC[0], D), F32)
        for seg in range(GROUPS):
            full = full + dot(vec_segs[seg].astype(LOW), spread_matrix(seg))
        rows_f32[...] = full

    def vector(row):
        return rows_f32[row : row + 1, :]

    def vector_tile(row, j):
        return rows_f32[row : row + 1, pl.ds(at128(j * TILE), TILE)]

    def block(n, j=None):
        start = n * D
        if not isinstance(n, int):
            start = at16(start)
        if j is None:
            return held[pl.ds(start, D), :]
        return held[pl.ds(start, D), pl.ds(at128(j * TILE), TILE)]

    def row_tiles(body):
        @pl.loop(0, rows // WIN)
        def _(i):
            body(pl.ds(at128(i * WIN), WIN), i)

    def col_tiles(body):
        @pl.loop(0, D // TILE)
        def _(j):
            body(pl.ds(at128(j * TILE), TILE), j)

    def norm_first():
        loads[0].wait()

        def one(here, i):
            unit, _ = normalized(chars_v[here, :].astype(F32))
            normed[here, :] = (unit * vector(A_GAIN) + vector(A_BIAS)).astype(LOW)

        row_tiles(one)

    def project_block(n):
        def one(here, j):
            value = dot(normed[...], block(QKV + n, j))
            if n == 0:
                value = value + vector_tile(Q_BIAS, j)
            if n == 2:
                value = value + vector_tile(V_BIAS, j)
            projected[n, :, here] = value.astype(LOW)

        col_tiles(one)

    def key_bias(w):
        code = codes[pl.ds(s * windows + w, 1), :]
        return jnp.where(code != 0, 0.0, mask_value).astype(F32)

    def lanes():
        return lax.broadcasted_iota(jnp.int32, (WIN, PAIR), 1) < HEAD_DIM

    def two_heads(values):
        first = lanes()
        zero = jnp.zeros_like(values)
        return jnp.concatenate(
            [jnp.where(first, values, zero), jnp.where(first, zero, values)], axis=0
        )

    def one_pair(values):
        return jnp.where(lanes(), values[:WIN], values[WIN:])

    scale_factor = HEAD_DIM ** (-0.5)

    def attend():
        def one(here, w):
            bias = key_bias(w)
            for p in range(PAIRS):
                cols = pl.ds(p * PAIR, PAIR)
                queries = two_heads(projected[0, here, cols])
                scores = dot_turned(queries, projected[1, here, cols]) * scale_factor + bias
                top = jnp.max(scores, axis=-1, keepdims=True)
                weight = jnp.exp(scores - top)
                weight = weight / jnp.sum(weight, axis=-1, keepdims=True)
                prob = weight.astype(LOW)
                probs[w, p] = prob
                context[here, cols] = one_pair(dot(prob, projected[2, here, cols])).astype(LOW)

        row_tiles(one)

    def attend_out():
        def one(here, j):
            value = dot(context[...], block(OUT, j)) + vector_tile(O_BIAS, j)
            hidden[:, here] = chars_v[:, here].astype(F32) + value

        col_tiles(one)

        def norm(here, i):
            unit, _ = normalized(hidden[here, :])
            normed_ffn[here, :] = (unit * vector(F_GAIN) + vector(F_BIAS)).astype(LOW)

        row_tiles(norm)

    def inner_block(n):
        def one(here, j):
            value = dot(normed_ffn[...], block(FIN + n, j)) + vector_tile(IN_BIAS + n, j)
            gelu, grad = gelu_parts(value)
            active[n, :, here] = gelu.astype(LOW)
            slope[n, :, here] = grad.astype(LOW)

        col_tiles(one)

    def by_place():
        i = lax.broadcasted_iota(jnp.int32, (WIN, WIN), 0)
        j = lax.broadcasted_iota(jnp.int32, (WIN, WIN), 1)
        return jnp.where(j == KERNEL * lax.rem(i, RUN) + i // RUN, 1.0, 0.0).astype(LOW)

    def layer_end():
        def one(here, j):
            value = hidden[:, here] + vector_tile(FO_BIAS, j)
            for n in range(BLOCKS):
                value = value + dot(active[n], block(FOUT + n, j))
            low_grad[:, here] = value.astype(LOW)

        col_tiles(one)
        order = by_place()

        def sort(here, w):
            moved = dot(order, low_grad[here, :]).astype(LOW)
            for k in range(KERNEL):
                stacked[k, pl.ds(at16(w * RUN), RUN), :] = moved[k * RUN : (k + 1) * RUN]

        row_tiles(sort)

    def note(row, value):
        vec_grads[row : row + 1, :] = value

    def note_more(row, value):
        vec_grads[row : row + 1, :] = vec_grads[row : row + 1, :] + value

    def convolve():
        loads[1].wait()
        value = jnp.zeros((mols, D), F32) + vector(C_BIAS)
        for k in range(KERNEL):
            value = value + dot(stacked[k], block(CONV + k))
        gelu, grad = gelu_parts(value)
        unit, scale = normalized(gelu)
        mol_v[...] = (unit * vector(D_GAIN) + vector(D_BIAS)).astype(LOW)
        wide = cot_v[...].astype(F32)
        note(D_GAIN, column_sum(wide * unit))
        note(D_BIAS, column_sum(wide))
        grad_conv = (norm_back(unit, scale, vector(D_GAIN), wide) * grad).astype(LOW)
        cot_v[...] = grad_conv
        note(C_BIAS, column_sum(grad_conv.astype(F32)))

    def convolve_back():
        for k in range(KERNEL):
            total[k * mols : (k + 1) * mols, :] = dot_turned(cot_v[...], block(CONV + k))

        for k in range(KERNEL):

            def one(here, j):
                value = dot_rows(stacked[k, :, here], cot_v[...])
                held[pl.ds(at128((CONV + k) * D + j * TILE), TILE), :] = value.astype(LOW)

            col_tiles(one)

        order = by_place()

        def sort(here, w):
            parts = [total[pl.ds(at16(k * mols + w * RUN), RUN), :] for k in range(KERNEL)]
            value = dot_rows(order, jnp.concatenate(parts, axis=0).astype(LOW))
            layer[here, :] = value
            low_grad[here, :] = value.astype(LOW)
            note_more(FO_BIAS, column_sum(value))

        row_tiles(sort)

    def weight_grad(n, left, right):
        def one(here, j):
            value = dot_rows(left[:, here], right[...])
            held[pl.ds(at128(n * D + j * TILE), TILE), :] = value.astype(LOW)

        col_tiles(one)

    def active_back(n):
        def one(here, j):
            value = dot_turned(
                low_grad[...], held[pl.ds(at128((FOUT + n) * D + j * TILE), TILE), :]
            )
            inner = (value * slope[n, :, here].astype(F32)).astype(LOW)
            slope[n, :, here] = inner
            vec_grads[IN_BIAS + n : IN_BIAS + n + 1, here] = column_sum(inner.astype(F32))

        col_tiles(one)
        weight_grad(FOUT + n, active.at[n], low_grad)

    def inner_sum():
        def one(here, j):
            value = jnp.zeros((rows, TILE), F32)
            for n in range(BLOCKS):
                value = value + dot_turned(
                    slope[n], held[pl.ds(at128((FIN + n) * D + j * TILE), TILE), :]
                )
            total[:, here] = value

        col_tiles(one)

    def hidden_back():
        def one(here, i):
            unit, scale = normalized(hidden[here, :])
            grad = total[here, :]
            note_more(F_GAIN, column_sum(grad * unit))
            note_more(F_BIAS, column_sum(grad))
            value = layer[here, :] + norm_back(unit, scale, vector(F_GAIN), grad)
            layer[here, :] = value
            low = value.astype(LOW)
            low_grad[here, :] = low
            note_more(O_BIAS, column_sum(low.astype(F32)))

        row_tiles(one)

    def context_back():
        def one(here, j):
            value = dot_turned(low_grad[...], held[pl.ds(at128(OUT * D + j * TILE), TILE), :])
            normed_ffn[:, here] = value.astype(LOW)

        col_tiles(one)
        weight_grad(OUT, context, low_grad)

    def attend_back():
        def one(here, w):
            for p in range(PAIRS):
                cols = pl.ds(p * PAIR, PAIR)
                grad_out = two_heads(normed_ffn[here, cols])
                prob = probs[w, p]
                wide = prob.astype(F32)
                grad_prob = dot_turned(grad_out, projected[2, here, cols])
                inner = jnp.sum(wide * grad_prob, axis=-1, keepdims=True)
                grad_score = (wide * (grad_prob - inner)).astype(LOW)
                grad_value = dot_rows(prob, grad_out)
                grad_query = one_pair(dot(grad_score, projected[1, here, cols])) * scale_factor
                grad_key = (
                    dot_rows(grad_score, two_heads(projected[0, here, cols])) * scale_factor
                )
                low_query, low_value = grad_query.astype(LOW), grad_value.astype(LOW)
                slope[0, here, cols] = low_query
                slope[1, here, cols] = grad_key.astype(LOW)
                slope[2, here, cols] = low_value
                for row, low in ((Q_BIAS, low_query), (V_BIAS, low_value)):
                    vec_grads[row : row + 1, cols] = vec_grads[row : row + 1, cols] + column_sum(
                        low.astype(F32)
                    )

        row_tiles(one)

    def project_sum():
        def one(here, j):
            value = jnp.zeros((rows, TILE), F32)
            for n in range(3):
                value = value + dot_turned(
                    slope[n], held[pl.ds(at128((QKV + n) * D + j * TILE), TILE), :]
                )
            total[:, here] = value

        col_tiles(one)

    def chars_back():
        def one(here, i):
            unit, scale = normalized(chars_v[here, :].astype(F32))
            grad = total[here, :]
            note_more(A_GAIN, column_sum(grad * unit))
            note_more(A_BIAS, column_sum(grad))
            value = layer[here, :] + norm_back(unit, scale, vector(A_GAIN), grad)
            context[here, :] = value.astype(LOW)

        row_tiles(one)

    def swap(i, whole, dst, count):
        keep = whole.at[:, pl.ds(at128(s * HALF), HALF)]
        give = whole.at[:, pl.ds(at128((1 - s) * HALF), HALF)]
        there = dst.at[pl.ds(at16(s * count), count)]
        stay = pltpu.make_async_copy(keep, there, io_sem.at[3 + i])
        go = remote(give, there, swap_send.at[i], swap_recv.at[i], near["x"])
        stay.start()
        go.start()
        return [stay, go]

    c = lax.rem(g, 2)
    y = g // 2
    mine, yours = 2 * y + c, 2 * (1 - y) + c

    def core_sum(k, i):
        return remote(
            held.at[pl.ds(spot(k, 2 * i + 1 - c), SHARD)],
            core_in.at[k, i],
            g_send.at[i, k],
            g_recv.at[i, k],
            near["c"],
        )

    def y_sum(k):
        return remote(
            held.at[pl.ds(spot(k, yours), SHARD)],
            y_in.at[k],
            g_send.at[2, k],
            g_recv.at[2, k],
            near["y"],
        )

    def part(k, side):
        return held.at[pl.ds(spot(k, mine), SHARD), pl.ds(at128(side * HALF), HALF)]

    def x_sum(k):
        return remote(part(k, 1 - s), x_in.at[k], g_send.at[3, k], g_recv.at[3, k], near["x"])

    def e_sum(k):
        return remote(part(k, s), e_in.at[k], g_send.at[4, k], g_recv.at[4, k], near["e"])

    def m_sum(k):
        return remote(part(k, s), m_in.at[k], g_send.at[5, k], g_recv.at[5, k], near["m"])

    def final(k):
        return shard_block(out, k, 0, SHARD, s * HALF, HALF)

    def e_back(k):
        return remote(part(k, s), final(k), g_send.at[6, k], g_recv.at[6, k], near["e"])

    def x_back(k, src):
        return remote(src, final(k), g_send.at[7, k], g_recv.at[7, k], near["x"])

    def own_back(k):
        return pltpu.make_async_copy(part(k, s), final(k), g_own.at[k])

    def sum_step(n, k):
        if n == 0:
            for i in range(2):
                core_sum(k, i).start()
        if n == 1:
            for i in range(2):
                core_sum(k, i).wait_recv()
                add_into(held, spot(k, 2 * i + c), SHARD, 0, D, core_in.at[k, i])
            y_sum(k).start()
        if n == 2:
            y_sum(k).wait_recv()
            add_into(held, spot(k, mine), SHARD, 0, D, y_in.at[k])
            x_sum(k).start()
        if n == 3:
            x_sum(k).wait_recv()
            add_into(held, spot(k, mine), SHARD, s * HALF, HALF, x_in.at[k])

            @pl.when(border)
            def _():
                e_sum(k).start()

        if n == 4:

            @pl.when(middle)
            def _():
                e_sum(k).wait_recv()
                add_into(held, spot(k, mine), SHARD, s * HALF, HALF, e_in.at[k])
                m_sum(k).start()

        if n == 5:

            @pl.when(middle)
            def _():
                m_sum(k).wait_recv()
                m_sum(k).wait_send()
                add_into(held, spot(k, mine), SHARD, s * HALF, HALF, m_in.at[k])
                for i in range(extra):
                    copy = remote(
                        part(k, s),
                        more_in.at[k, i],
                        more_send.at[k, i],
                        more_recv.at[k, i],
                        far[i],
                    )
                    copy.start()
                    copy.wait()
                    copy = pltpu.make_async_copy(more_in.at[k, i], e_in.at[k], g_own.at[k])
                    copy.start()
                    copy.wait()
                    add_into(held, spot(k, mine), SHARD, s * HALF, HALF, e_in.at[k])
                own_back(k).start()
                e_back(k).start()
                x_back(k, part(k, s)).start()

        if n == 6:

            @pl.when(border)
            def _():
                e_back(k).wait_recv()
                x_back(k, final(k)).start()

    def sums_done():
        for k in range(COUNT):
            for i in range(2):
                core_sum(k, i).wait_send()
            y_sum(k).wait_send()
            x_sum(k).wait_send()

            @pl.when(border)
            def _():
                e_sum(k).wait_send()

            @pl.when(middle)
            def _():
                own_back(k).wait()
                e_back(k).wait_send()

            x_back(k, part(k, s)).wait()

    vec_steps = 6 + extra
    vec_moves = []

    def vec_step(n):
        if n == 0:
            top = vec_grads[...]
            high = top.astype(LOW)
            low = (top - high.astype(F32)).astype(LOW)
            for seg in range(GROUPS):
                spread = spread_matrix(seg)
                vec_segs[seg] = dot_turned(high, spread) + dot_turned(low, spread)
            for row, parts in SEGMENTS.items():
                for seg, (q, at) in enumerate(parts):
                    vecs[q, at : at + 1, :] = vec_segs[seg, row : row + 1, :]
            for i in range(2):
                copy = remote(
                    vecs.at[2 * i + 1 - c], vec_in.at[i], v_send.at[3 + i], v_recv.at[3 + i], near["c"]
                )
                copy.start()
                vec_moves.append(copy)
            return
        if n == 1:
            for i in range(2):
                vec_moves[i].wait()
                vecs[2 * i + c] = vecs[2 * i + c] + vec_in[i]
        else:
            vec_moves[-1].wait()
            vecs[mine] = vecs[mine] + vec_in[n]
        steps = [near["y"], near["x"], near["e"], near["w"]] + far
        if n <= len(steps):
            copy = remote(
                vecs.at[yours if n == 1 else mine],
                vec_in.at[1 + n],
                v_send.at[4 + n],
                v_recv.at[4 + n],
                steps[n - 1],
            )
            copy.start()
            vec_moves.append(copy)
        else:
            copy = pltpu.make_async_copy(vecs.at[mine], vec_out, io_sem.at[2])
            copy.start()
            copy.wait()

    vec_grads[...] = jnp.zeros_like(vec_grads)
    gather_step(0)
    vectors_ready()
    gather_step(1)
    norm_first()
    forward = [
        ([0], lambda: project_block(0)),
        ([1], lambda: project_block(1)),
        ([2], lambda: project_block(2)),
        ([], attend),
        ([3], attend_out),
    ]
    forward += [([FIN + n], functools.partial(inner_block, n)) for n in range(BLOCKS)]
    forward += [([8, 9, 10, 11], layer_end), ([12, 13, 14, 15], convolve)]
    for step in range(2, COUNT + x_lag):
        gather_step(step)
        while forward and all(k <= step - x_lag - 1 for k in forward[0][0]):
            need, work = forward.pop(0)
            for k in need:
                weight_ready(k)
            work()
    for need, work in forward:
        for k in need:
            weight_ready(k)
        work()
    gather_done()

    order = [12, 13, 14, 15, 8, 9, 10, 11, 4, 5, 6, 7, 3, 0, 1, 2]
    lags = [0, 1, 2, 3, 4, 5, 6]
    progress = {"at": 0}

    def advance(ready):
        while progress["at"] < ready:
            i = progress["at"]
            for n in reversed(range(len(lags))):
                j = i - lags[n]
                if 0 <= j < COUNT:
                    sum_step(n, order[j])
            progress["at"] = i + 1

    convolve_back()
    moves = swap(0, mol_v, mols_out, mols)
    advance(1)
    active_back(0)
    advance(2)
    active_back(1)
    advance(3)
    active_back(2)
    advance(4)
    active_back(3)
    advance(5)
    inner_sum()
    advance(6)
    for n in range(BLOCKS):
        weight_grad(FIN + n, normed_ffn, slope.at[n])
    advance(7)
    hidden_back()
    context_back()
    advance(8)
    attend_back()
    advance(9)
    project_sum()
    for n in range(3):
        weight_grad(QKV + n, normed, slope.at[n])
    advance(10)
    chars_back()
    moves += swap(1, context, chars_out, rows)
    for i in range(vec_steps):
        advance(11 + i)
        vec_step(i)
    advance(COUNT + lags[-1])
    sums_done()
    for copy in moves:
        copy.wait()


def run(args, chars, extra):
    rows = chars.shape[0] // 2
    mols = rows // KERNEL
    anywhere = pl.BlockSpec(memory_space=pl.ANY)
    dma = pltpu.SemaphoreType.DMA
    vmem = pltpu.VMEM
    windows = rows // WIN
    return pl.pallas_call(
        functools.partial(program_kernel, rows, extra),
        name="layer_and_sums",
        out_shape=[
            jax.ShapeDtypeStruct((2 * mols, HALF), LOW),
            jax.ShapeDtypeStruct((2 * rows, HALF), LOW),
            jax.ShapeDtypeStruct(VEC, F32),
        ]
        + [jax.ShapeDtypeStruct(shape, LOW) for shape in SHARD_SHAPES]
        + [jax.ShapeDtypeStruct((COUNT, extra, SHARD, HALF), LOW)] * (extra > 0),
        in_specs=[anywhere, pl.BlockSpec(memory_space=vmem)] + [anywhere] * 7,
        out_specs=[anywhere] * (8 + (extra > 0)),
        scratch_shapes=[
            vmem((COUNT * D, D), LOW),
            vmem((COUNT, 2, SHARD, D), LOW),
            vmem((COUNT, SHARD, D), LOW),
            vmem((COUNT, SHARD, HALF), LOW),
            vmem((COUNT, SHARD, HALF), LOW),
            vmem((COUNT, SHARD, HALF), LOW),
            vmem((GROUPS,) + VEC, F32),
            vmem((GROUPS,) + VEC, F32),
            vmem((VEC[0], D), F32),
            vmem((VEC[0], D), F32),
            vmem((7 + extra,) + VEC, F32),
            vmem((rows, D), LOW),
            vmem((mols, D), LOW),
            vmem((rows, D), LOW),
            vmem((3, rows, D), LOW),
            vmem((windows, PAIRS, 2 * WIN, WIN), LOW),
            vmem((rows, D), LOW),
            vmem((rows, D), F32),
            vmem((rows, D), LOW),
            vmem((BLOCKS, rows, D), LOW),
            vmem((BLOCKS, rows, D), LOW),
            vmem((rows, D), F32),
            vmem((KERNEL, mols, D), LOW),
            vmem((rows, D), LOW),
            vmem((rows, D), F32),
            vmem((mols, D), LOW),
            dma((5, COUNT)),
            dma((5, COUNT)),
            dma((COUNT,)),
            dma((8, COUNT)),
            dma((8, COUNT)),
            dma((COUNT,)),
            dma((COUNT, max(extra, 1))),
            dma((COUNT, max(extra, 1))),
            dma((9 + extra,)),
            dma((9 + extra,)),
            dma((5,)),
            dma((2,)),
            dma((2,)),
        ],
        compiler_params=pltpu.CompilerParams(
            collective_id=0, has_side_effects=True, vmem_limit_bytes=63 << 20
        ),
    )(*args)


VEC_COUNTS = [1, 1, 2, 1, 1, 1, 4, 1, 1, 1, 1]


def body(
    chars,
    char_codes,
    mol_cotangent,
    attn_norm_gain,
    attn_norm_bias,
    qkv_weight,
    qv_bias,
    out_weight,
    out_bias,
    ffn_norm_gain,
    ffn_norm_bias,
    ffn_in_weight,
    ffn_in_bias,
    ffn_out_weight,
    ffn_out_bias,
    conv_weight,
    conv_bias,
    down_norm_gain,
    down_norm_bias,
):
    vectors = [
        attn_norm_gain,
        attn_norm_bias,
        qv_bias,
        out_bias,
        ffn_norm_gain,
        ffn_norm_bias,
        ffn_in_bias,
        ffn_out_bias,
        conv_bias,
        down_norm_gain,
        down_norm_bias,
    ]
    packed = jnp.concatenate([v.reshape(-1, SHARD) for v in vectors], axis=0).astype(F32)
    packed = jnp.pad(packed, ((0, VEC[0] - packed.shape[0]), (0, VEC[1] - SHARD)))
    result = run(
        (
            chars,
            char_codes.reshape(-1, WIN),
            mol_cotangent,
            packed,
            qkv_weight,
            out_weight,
            ffn_in_weight,
            ffn_out_weight,
            conv_weight,
        ),
        chars,
        (lax.axis_size("replica") // RING).bit_length() - 1,
    )
    molecules, chars_grad, vec_sum = result[:3]
    t_qkv, t_out, t_in, t_ffo, t_conv = [w.astype(F32) for w in result[3:8]]
    v = []
    row = 0
    for count in VEC_COUNTS:
        v.append(vec_sum[row : row + count, :SHARD].reshape(-1))
        row += count
    return (
        molecules,
        chars_grad,
        v[0],
        v[1],
        t_qkv,
        v[2],
        t_out,
        v[3],
        v[4],
        v[5],
        t_in,
        v[6],
        t_ffo,
        v[7],
        t_conv,
        v[8],
        v[9],
        v[10],
    )


def solution(mesh):
    return jax.shard_map(
        body,
        mesh=mesh,
        in_specs=(
            P(("group", "replica"), None),
            P(("group", "replica")),
            P(("group", "replica"), None),
            P("group"),
            P("group"),
            P("group", None),
            P("group"),
            P("group", None),
            P("group"),
            P("group"),
            P("group"),
            P("group", None),
            P("group"),
            P("group", None),
            P("group"),
            P("group", None),
            P("group"),
            P("group"),
            P("group"),
        ),
        out_specs=(
            P(("group", "replica"), "section"),
            P(("group", "replica"), "section"),
            P("group"),
            P("group"),
            P("group", None),
            P("group"),
            P("group", None),
            P("group"),
            P("group"),
            P("group"),
            P("group", None),
            P("group"),
            P("group", None),
            P("group"),
            P("group", None),
            P("group"),
            P("group"),
            P("group"),
        ),
        check_vma=False,
    )
```

time: 1130 us -> 246 us (0.22)
  blocking collectives: 406 us -> 0 us
  waiting for transfers between devices: 332 us -> 0 us
  Pallas kernels: 0 us -> 222 us
  matrix products: 188 us -> 0 us
  local copies, waits for them, and re-layouts: 119 us -> 13.5 us
  other arithmetic: 44.5 us -> 8.97 us
  between operations: 17.8 us -> 0.68 us
    psum x1 -> x0, blocking collectives: 371 us -> none  [body(): totals = lax.psum(shard_sums, ('section', 'replica'))]
    pallas_call x0 -> x1, Pallas kernels: none -> 222 us  [run(): pl.pallas_call(functools.partial(program_kernel, rows, extra), name='laye...]
    dot_general x38 -> x0, matrix products: 188 us -> none  [the longest x8 61.6 us: project(): return jnp.dot(left_side, right_side, preferred_element_type=jnp.float32)]
    reduce_scatter x5 -> x0, waiting for transfers between devices: 167 us -> none  [body(): lax.psum_scatter(as_sent(all_sums), 'group', scatter_dimension=0, tiled=T...]
    all_gather x5 -> x0, waiting for transfers between devices: 102 us -> none  [the longest x1 39.1 us: body(): lax.all_gather(ffn_in_weight, 'group', axis=0, tiled=True)]
    ppermute x6 -> x0, waiting for transfers between devices: 59.7 us -> none  [the longest x4 52.5 us: from_behind(): return lax.ppermute(block, axis, route)]
    cond x136 -> x0, local copies, waits for them, and re-layouts: 34.7 us -> none  [the longest x4 26.7 us: body(): lax.cond(is_first, first_section, last_section)]
    another operation x11 -> x0, local copies, waits for them, and re-layouts: 25.7 us -> none
  transfers between devices with their start and end apart: 16 -> 0, of which waited for: 13 -> 0; matrix products, arithmetic and copies ran while one was open for 8% -> 0% of each run, Pallas kernels for 0% -> 0%
where the time goes in v2:
time: 246 us
  Pallas kernels  222 us (90%)
  local copies, waits for them, and re-layouts  13.5 us (5%)
  other arithmetic  8.97 us (4%)
    pallas_call x1, Pallas kernels, run(): pl.pallas_call(functools.partial(program_kernel, rows, extra), name='laye...  222 us
    convert_element_type x5, other arithmetic, body(): t_qkv, t_out, t_in, t_ffo, t_conv = [w.astype(F32) for w in result[3:8]]  8.36 us
    reshape x11, local copies, waits for them, and re-layouts, body(): v.reshape(-1, SHARD)  7.45 us

profile of v2, /device:TPU:0, one launch (start us, length us, event | category | flops | bytes accessed | tf_op | source)
XLA Modules:
  0.0 245.6 jit_solution(957196703635220924)
XLA Ops:
  0.7 0.8 reshape.112
  1.4 0.7 reshape.106
  2.1 0.7 reshape.107
  2.7 0.8 reshape.108
  3.5 0.7 reshape.109
  4.2 0.7 reshape.110
  4.8 0.7 reshape.111
  5.5 0.7 reshape.113
  6.1 0.7 reshape.114
  6.8 0.7 reshape.115
  7.5 0.7 reshape.116
  8.9 222.5 %layer_and_sums.1 = (bf16[256,384]{1,0:T(8,128)(2,1)}, bf16[1024,384]{1,0:T(8,128)(2,1)}, f32[16,256]{1,0:T(8,128)}, bf16[192,2304]{1,0:T(8,128)(2,1)}, bf16[192...) custom-call(bf16[1024,768]{1,0:T(8,128)(2,1)} %refs_0_.1, ...), custom_call_target="tpu_custom_call" | custom-call | tf_op jit(solution)/shard_map/layer_and_sums/pallas_call | solution.py:861
  231.3 1.5 fusion
  232.8 0.7 slice.39
  233.5 0.7 reshape.123
  234.2 0.7 slice.35
  234.9 0.7 reshape.119
  235.6 3.0 %convert_element_type.20 = f32[192,3072]{1,0:T(8,128)} convert(bf16[192,3072]{1,0:T(8,128)(2,1)} %get-tuple-element.31) | non-fusion elementwise | flops 589824 | bytes 3538944 | tf_op jit(solution)/shard_map/convert_element_type | solution.py:975
  238.6 1.6 convert_element_type.21
  240.3 1.6 convert_element_type.22
  241.9 1.3 convert_element_type.18
  243.2 0.9 convert_element_type.19
  244.0 0.7 copy.39
  244.7 0.9 copy.40
  (14 shorter events, 0.9 us)
Async XLA Ops:
  235.6 3.0 %copy-start.1 = (bf16[768,768]{1,0:T(8,128)(2,1)S(1)}, bf16[768,768]{1,0:T(8,128)(2,1)}, u32[]{:S(2)}) copy-start(bf16[768,768]{1,0:T(8,128)(2,1)} %get-tuple-element.32) | copy-start | bytes 3538948
  238.6 1.7 copy-start
  240.3 1.6 copy-start.2
  241.9 1.3 copy-start.4
  241.9 2.2 copy-start.5
  243.2 1.5 copy-start.3
